TPU v7x, 256 devices: a whole 4x4x8 slice. The times are simulated.
256 devices in a mesh: learn: 8 (over z_hi, x), tp: 16 (over y, z_lo), dp: 2 (over core).
Axes of the slice: x: 4, y: 4, z: 8 (z_hi: 2, z_lo: 4; z = z_hi * 4 + z_lo), core: 2. Of those that a mesh axis runs over, the one named last changes fastest.
Arguments:
- gradient: bfloat16 [29568, 8192], P('tp', ('learn', 'dp')), may hold values from -6 to 6
- frame_basis: bfloat16 [8192, 1024], P(('learn', 'dp')), may hold values from -0.0625 to 0.0625
- moment_first: float32 [29568, 1024], P('tp', ('learn', 'dp')), may hold values from -3 to 3
- moment_second: float32 [29568, 1024], P('tp', ('learn', 'dp')), may hold values from 0.05 to 1
- refresh: int32 [1024], P(('learn', 'dp')), may hold values 0 or 1
- old_weight: bfloat16 [29568, 8192], P('tp', ('learn', 'dp')), may hold values from -0.03125 to 0.03125
- hidden: bfloat16 [128, 29568], P('dp', 'tp'), may hold values from -6 to 6
Outputs:
- new_first: float32 [29568, 1024], P('tp', ('learn', 'dp'))
- new_second: float32 [29568, 1024], P('tp', ('learn', 'dp'))
- new_weight: bfloat16 [29568, 8192], P('tp', ('learn', 'dp'))
- mlp_out: bfloat16 [128, 8192], P('dp', ('learn', 'tp'))
All inputs are finite; a program needn't handle non-finite values. No bound on the sum of `refresh` on one device may be relied on, other than what follows from the above.
Results may differ from a plain program's by a relative error of at most 0.0075.
Values may be sent and summed in bfloat16 or wider, within the bound.
No kernel may reach another device: no remote copies, remote signals or barrier semaphores. Data moves between devices by JAX's collectives and lax.ppermute only.
A program may use at most 64 MiB of HBM per device.

v0:
```python
import jax
import jax.numpy as jnp
from jax import lax
from jax.sharding import PartitionSpec as P

BETA_ONE = 0.9
BETA_TWO = 0.999
ADAM_EPS = 1e-06
STEP_RATE = 0.01


def shards(gradient, frame_basis, moment_first, moment_second, refresh, old_weight, hidden):
    partial_low = jnp.dot(gradient, frame_basis, preferred_element_type=jnp.float32)
    projected = lax.psum_scatter(partial_low, ("learn", "dp"), scatter_dimension=1, tiled=True)
    fresh = (refresh == 1)[None, :]
    start_first = jnp.where(fresh, jnp.float32(0.0), moment_first)
    start_second = jnp.where(fresh, jnp.float32(0.0), moment_second)
    new_first = BETA_ONE * start_first + (1.0 - BETA_ONE) * projected
    new_second = BETA_TWO * start_second + (1.0 - BETA_TWO) * projected * projected
    ratio = (new_first / (jnp.sqrt(new_second) + ADAM_EPS)).astype(jnp.bfloat16)
    delta = lax.dot_general(
        lax.all_gather(ratio, ("learn", "dp"), axis=1, tiled=True),
        frame_basis,
        (((1,), (1,)), ((), ())),
        preferred_element_type=jnp.float32,
    )
    new_weight = (old_weight.astype(jnp.float32) - STEP_RATE * delta).astype(jnp.bfloat16)
    row_terms = jnp.dot(
        hidden,
        lax.all_gather(new_weight, "dp", axis=1, tiled=True),
        preferred_element_type=jnp.float32,
    )
    mlp_out = lax.psum_scatter(row_terms, "tp", scatter_dimension=1, tiled=True).astype(
        jnp.bfloat16
    )
    return (new_first, new_second, new_weight, mlp_out)


def solution(mesh):
    placed = (
        P("tp", ("learn", "dp")),
        P(("learn", "dp"), None),
        P("tp", ("learn", "dp")),
        P("tp", ("learn", "dp")),
        P(("learn", "dp")),
        P("tp", ("learn", "dp")),
        P("dp", "tp"),
    )
    return jax.shard_map(
        shards,
        mesh=mesh,
        in_specs=placed,
        out_specs=(
            P("tp", ("learn", "dp")),
            P("tp", ("learn", "dp")),
            P("tp", ("learn", "dp")),
            P("dp", ("learn", "tp")),
        ),
        check_vma=False,
    )
```

profile of v0, /device:TPU:6, one launch (start us, length us, event | category | flops | bytes accessed | tf_op | source)
XLA Modules:
  0.0 344.9 jit_solution(3487945665392837278)
XLA Ops:
  7.2 0.0 copy-start
  7.2 0.0 reduce-scatter.5.cloned.1.call-start
  7.2 1.5 copy-done
  8.7 6.7 %fusion.2 = f32[1848,1024]{0,1:T(8,128)} fusion(bf16[1848,512]{1,0:T(8,128)(2,1)S(1)} %copy-done, bf16[512,1024]{1,0:T(8,128)(2,1)} %param.8), kind=kOutput, calls=%fused_computation.7 | convolution fusion | flops 1937768448 | bytes 10510336 | tf_op jit(solution)/shard_map/dot_general | solution.py:13
  15.4 0.0 reduce-scatter.5.cloned.1.call-update
  15.4 0.0 all-gather.3.cloned.1.call-start
  15.4 0.6 copy-done.4
  16.0 135.3 %reduce-scatter.5.cloned.1.call-done = f32[1848,64]{0,1:T(8,128)} async-done(((f32[1848,1024]{0,1:T(8,128)}), f32[1848,64]{0,1:T(8,128)}) %reduce-scatter.5.cloned.1.call-update) | async-done | bytes 473104 | tf_op jit(solution)/shard_map/reduce_scatter | solution.py:14
  151.3 0.0 copy-done.1
  151.3 0.0 copy-done.2
  151.3 2.3 divide_convert_fusion
  153.6 0.0 all-gather.3.cloned.1.call-update
  153.6 0.0 copy-start.3
  153.6 0.0 all-gather.5.cloned.1.call-start
  153.7 72.0 %all-gather.3.cloned.1.call-done = bf16[1848,1024]{0,1:T(8,128)(2,1)} async-done(((bf16[1848,64]{0,1:T(8,128)(2,1)}), bf16[1848,1024]{0,1:T(8,128)(2,1)}) %all-gather.3.cloned.1.call-update) | async-done | bytes 3784720 | tf_op jit(solution)/shard_map/all_gather | solution.py:22
  225.7 6.7 %subtract_convert_fusion = bf16[1848,512]{1,0:T(8,128)(2,1)} fusion(bf16[1848,512]{1,0:T(8,128)(2,1)} %param.12, bf16[1848,1024]{0,1:T(8,128)(2,1)} %all-gather.3.cloned.1.call-done, bf16[512,1024]{1,0:T(8,128)(2,1)} %param.8), kind=kOutput, calls=%fused_computation | convolution fusion | flops 1941553152 | bytes 8617984 | tf_op jit(solution)/shard_map/dot_general | solution.py:21
  232.3 0.0 all-gather.5.cloned.1.call-update
  232.4 0.0 reduce-scatter.7.cloned.1.call-start
  232.4 14.3 %all-gather.5.cloned.1.call-done = bf16[1848,1024]{1,0:T(8,128)(2,1)} async-done(((bf16[1848,512]{1,0:T(8,128)(2,1)}), bf16[1848,1024]{1,0:T(8,128)(2,1)}) %all-gather.5.cloned.1.call-update) | async-done | bytes 3784720 | tf_op jit(solution)/shard_map/all_gather | solution.py:30
  246.8 2.9 convolution_bitcast_fusion
  249.6 1.0 copy.11
  250.7 0.0 reduce-scatter.7.cloned.1.call-update
  250.7 86.3 %reduce-scatter.7.cloned.1.call-done = f32[64,64]{1,0:T(8,128)} async-done(((f32[1024,64]{1,0:T(8,128)}), f32[64,64]{1,0:T(8,128)}) %reduce-scatter.7.cloned.1.call-update) | async-done | bytes 16400
  336.9 1.4 copy.12
  (5 shorter events, 0.0 us)
Async XLA Ops:
  7.2 1.5 copy-start
  7.2 144.1 %reduce-scatter.5.cloned.1.call-start = ((), (), s32[]{:S(2)}) async-start(), calls=%async_computation.2 | async-start | bytes 8355840 | tf_op jit(solution)/shard_map/reduce_scatter | solution.py:14
  15.4 0.7 copy-start.4
  15.4 136.0 %copy-start.1 = (f32[1848,64]{0,1:T(8,128)S(1)}, f32[1848,64]{0,1:T(8,128)}, u32[]{:S(2)}) copy-start(f32[1848,64]{0,1:T(8,128)} %param.10) | copy-start | bytes 1419268
  15.4 136.0 %copy-start.2 = (f32[1848,64]{0,1:T(8,128)S(1)}, f32[1848,64]{0,1:T(8,128)}, u32[]{:S(2)}) copy-start(f32[1848,64]{0,1:T(8,128)} %param.9) | copy-start | bytes 1419268
  15.4 210.3 %all-gather.3.cloned.1.call-start = ((), (), s32[]{:S(2)}) async-start(), calls=%async_computation.3 | async-start | bytes 4177920 | tf_op jit(solution)/shard_map/all_gather | solution.py:22
  153.6 93.1 %copy-start.3 = (bf16[64,1848]{1,0:T(8,128)(2,1)S(1)}, bf16[64,1848]{1,0:T(8,128)(2,1)}, u32[]{:S(2)}) copy-start(bf16[64,1848]{1,0:T(8,128)(2,1)} %param.13) | copy-start | bytes 709636
  153.6 93.1 %all-gather.5.cloned.1.call-start = ((), (), s32[]{:S(2)}) async-start(), calls=%async_computation.4 | async-start | bytes 5677056 | tf_op jit(solution)/shard_map/all_gather | solution.py:30
  232.4 104.6 %reduce-scatter.7.cloned.1.call-start = ((), (), s32[]{:S(2)}) async-start(), calls=%async_computation.5 | async-start | bytes 557056
Sparse Core Ops, SparseCore 0:
  15.5 135.7 reduce-scatter.4
  154.6 71.0 all-gather.2
  232.5 14.2 all-gather.4
  250.8 86.0 reduce-scatter.6
where the time goes:
time: 345 us
  waiting for transfers between devices  308 us (89%)
  matrix products  16.2 us (5%)
  between operations  13.8 us (4%)
  local copies, waits for them, and re-layouts  4.52 us (1%)
    reduce_scatter x1, waiting for transfers between devices, shards(): lax.psum_scatter(partial_low, ('learn', 'dp'), scatter_dimension=1, tiled...  135 us
    unnamed x5, waiting for transfers between devices  86.3 us
    all_gather x1, waiting for transfers between devices, shards(): lax.all_gather(ratio, ('learn', 'dp'), axis=1, tiled=True)  72 us
    all_gather x1, waiting for transfers between devices, shards(): lax.all_gather(new_weight, 'dp', axis=1, tiled=True)  14.3 us
  transfers between devices with their start and end apart: 4, of which 4 were waited for; matrix products, arithmetic and copies ran while one was open for 0% of the time, Pallas kernels for 0%

commit v1 on v0

v1 whole, which is shorter than its diff:
```python
import functools

import jax
import jax.numpy as jnp
from jax import lax
from jax.experimental import pallas as pl
from jax.experimental.pallas import tpu as pltpu
from jax.sharding import PartitionSpec as P

BETA_ONE = 0.9
BETA_TWO = 0.999
ADAM_EPS = 1e-06
STEP_RATE = 0.01
RING = 4
CHUNKS = 2
ROWS = 256
F32 = jnp.float32
BF16 = jnp.bfloat16


def arrange_kernel(where_ref, basis_ref, own_ref, other_ref, turned):
    zh, x, d = where_ref[0], where_ref[1], where_ref[2]
    width = turned.shape[0] // 16
    turned[...] = basis_ref[...].T
    for side, out_ref in ((0, own_ref), (1, other_ref)):
        for j in range(RING):
            for zrel in range(2):
                block = ((zh ^ zrel) * RING + ((x + j) & (RING - 1))) * 2 + (d ^ side)
                first = (2 * j + zrel) * width
                out_ref[first : first + width, :] = turned[
                    pl.ds(pl.multiple_of(block * width, width), width), :
                ]


def arrange(where, basis):
    depth, rank = basis.shape
    out = jax.ShapeDtypeStruct((rank // 2, depth), basis.dtype)
    return pl.pallas_call(
        arrange_kernel,
        grid_spec=pltpu.PrefetchScalarGridSpec(
            num_scalar_prefetch=1,
            grid=(1,),
            in_specs=[pl.BlockSpec((depth, rank), lambda i, w: (0, 0))],
            out_specs=[pl.BlockSpec((rank // 2, depth), lambda i, w: (0, 0))] * 2,
            scratch_shapes=[pltpu.VMEM((rank, depth), basis.dtype)],
        ),
        out_shape=(out, out),
        cost_estimate=pl.CostEstimate(flops=0, bytes_accessed=8 * depth * rank, transcendentals=0),
    )(where, basis)


def project_kernel(own_ref, other_ref, mine_ref, theirs_ref, *outs):
    contract = (((1,), (1,)), ((), ()))
    low = lax.dot_general(own_ref[...], mine_ref[...], contract, preferred_element_type=F32)
    low += lax.dot_general(other_ref[...], theirs_ref[...], contract, preferred_element_type=F32)
    width = low.shape[0] // 8
    for k, out_ref in enumerate(outs):
        out_ref[...] = low[k * width : (k + 1) * width].astype(out_ref.dtype)


def project(basis_own, basis_other, gradient, theirs, first, count):
    ranks, depth = basis_own.shape
    width = ranks // 8
    steps = pl.cdiv(count, ROWS)
    start = first // ROWS
    return pl.pallas_call(
        project_kernel,
        grid=(steps,),
        in_specs=[
            pl.BlockSpec((ranks, depth), lambda i: (0, 0)),
            pl.BlockSpec((ranks, depth), lambda i: (0, 0)),
            pl.BlockSpec((ROWS, depth), lambda i: (start + i, 0)),
            pl.BlockSpec((ROWS, depth), lambda i: (i, 0)),
        ],
        out_specs=[pl.BlockSpec((width, ROWS), lambda i: (0, i))] * 8,
        out_shape=[
            jax.ShapeDtypeStruct((width, count), F32) for k in range(8)
        ],
        cost_estimate=pl.CostEstimate(
            flops=4 * ranks * depth * count, bytes_accessed=8 * depth * count, transcendentals=0
        ),
    )(basis_own, basis_other, gradient, theirs)


def update_kernel(first, limit, has_weight, *refs):
    if has_weight:
        refs = refs[1:]
    (mine_ref, theirs_ref, own_ref, other_ref, old_ref, hid_ref, hid_far_ref, sum_ref, new_ref, out_ref) = refs
    i = pl.program_id(0)
    contract = (((0,), (0,)), ((), ()))
    delta = lax.dot_general(mine_ref[...], own_ref[...], contract, preferred_element_type=F32)
    delta += lax.dot_general(theirs_ref[...], other_ref[...], contract, preferred_element_type=F32)
    new = (old_ref[...].astype(F32) - STEP_RATE * delta).astype(BF16)
    new_ref[...] = new
    left = limit - first - i * ROWS
    new = jnp.where(lax.broadcasted_iota(jnp.int32, new.shape, 0) < left, new, jnp.zeros_like(new))
    hid = jnp.concatenate([hid_ref[...], hid_far_ref[...]], axis=0)
    hid = jnp.where(lax.broadcasted_iota(jnp.int32, hid.shape, 1) < left, hid, jnp.zeros_like(hid))

    @pl.when(i == 0)
    def _():
        out_ref[...] = sum_ref[...]

    out_ref[...] += jnp.dot(hid, new, preferred_element_type=F32)


def update(weight, mine, theirs, basis_own, basis_other, old, hid, hid_far, total, first, count):
    ranks, depth = basis_own.shape
    rows = old.shape[0]
    seqs = hid.shape[0]
    steps = pl.cdiv(count, ROWS)
    start = first // ROWS
    in_specs = [
        pl.BlockSpec((ranks, ROWS), lambda i: (0, i)),
        pl.BlockSpec((ranks, ROWS), lambda i: (0, i)),
        pl.BlockSpec((ranks, depth), lambda i: (0, 0)),
        pl.BlockSpec((ranks, depth), lambda i: (0, 0)),
        pl.BlockSpec((ROWS, depth), lambda i: (start + i, 0)),
        pl.BlockSpec((seqs, ROWS), lambda i: (0, start + i)),
        pl.BlockSpec((seqs, ROWS), lambda i: (0, start + i)),
        pl.BlockSpec((2 * seqs, depth), lambda i: (0, 0)),
    ]
    args = (mine, theirs, basis_own, basis_other, old, hid, hid_far, total)
    aliases = {}
    if weight is not None:
        in_specs = [pl.BlockSpec(memory_space=pl.ANY)] + in_specs
        args = (weight,) + args
        aliases = {0: 0}
    return pl.pallas_call(
        functools.partial(update_kernel, first, rows, weight is not None),
        grid=(steps,),
        in_specs=in_specs,
        out_specs=[
            pl.BlockSpec((ROWS, depth), lambda i: (start + i, 0)),
            pl.BlockSpec((2 * seqs, depth), lambda i: (0, 0)),
        ],
        out_shape=[
            jax.ShapeDtypeStruct((rows, depth), BF16),
            jax.ShapeDtypeStruct((2 * seqs, depth), F32),
        ],
        input_output_aliases=aliases,
        cost_estimate=pl.CostEstimate(
            flops=4 * ranks * depth * count, bytes_accessed=8 * depth * count, transcendentals=0
        ),
    )(*args)


def shards(gradient, frame_basis, moment_first, moment_second, refresh, old_weight, hidden):
    learn = lax.axis_index("learn")
    where = jnp.stack([learn // RING, learn % RING, lax.axis_index("dp")]).astype(jnp.int32)
    up = [(z * RING + x, z * RING + (x + 1) % RING) for z in range(2) for x in range(RING)]
    down = [(b, a) for a, b in up]
    across = [(i, (i + RING) % (2 * RING)) for i in range(2 * RING)]
    plus = lambda v: lax.ppermute(v, "learn", up)
    minus = lambda v: lax.ppermute(v, "learn", down)
    far = lambda v: lax.ppermute(v, "learn", across)
    twin = lambda v: lax.ppermute(v, "dp", [(0, 1), (1, 0)])

    rows = gradient.shape[0]
    size = -(-rows // (CHUNKS * ROWS)) * ROWS
    cuts = [(a, min(size, rows - a)) for a in range(0, rows, size)]

    basis_own, basis_send = arrange(where, frame_basis)
    basis_recv = twin(basis_send)
    hid_far = twin(hidden)
    first_t, second_t = moment_first.T, moment_second.T
    fresh = (refresh == 1)[:, None]

    ratios = []
    firsts, seconds = [], []
    for a, n in cuts:
        theirs = twin(gradient[a : a + n])
        p00, p01, p10, p11, p20, p21, p30, p31 = project(basis_own, basis_recv, gradient, theirs, a, n)
        from_low = plus(p20)
        from_high = minus(p21)
        low1 = plus(p11)
        high0 = minus(p30)
        low0 = plus(p10 + from_low)
        high1 = minus(p31 + from_high)
        keep = p00 + low0 + high0
        give = p01 + low1 + high1
        projected = keep + far(give)
        start_first = jnp.where(fresh, F32(0.0), first_t[:, a : a + n])
        start_second = jnp.where(fresh, F32(0.0), second_t[:, a : a + n])
        new_first = BETA_ONE * start_first + (1.0 - BETA_ONE) * projected
        new_second = BETA_TWO * start_second + (1.0 - BETA_TWO) * projected * projected
        ratio = (new_first / (jnp.sqrt(new_second) + ADAM_EPS)).astype(BF16)
        firsts.append(new_first)
        seconds.append(new_second)
        ratios.append(ratio)

    weight = None
    total = jnp.zeros((2 * hidden.shape[0], old_weight.shape[1]), F32)
    for (a, n), r0 in zip(cuts, ratios):
        rz = far(r0)
        m0 = plus(r0)
        q0 = minus(r0)
        t0 = plus(m0)
        mz = plus(rz)
        qz = minus(rz)
        tz = minus(qz)
        mine = jnp.concatenate([r0, rz, q0, qz, t0, tz, m0, mz], axis=0)
        theirs = twin(mine)
        weight, total = update(
            weight, mine, theirs, basis_own, basis_send, old_weight, hidden, hid_far, total, a, n
        )

    seqs = hidden.shape[0]
    near, away = total[:seqs], twin(total[seqs:])
    d = lax.axis_index("dp")
    pair = jnp.where(d == 0, jnp.stack([near, away]), jnp.stack([away, near]))
    cols = frame_basis.shape[0] // 8
    parts = pair.reshape(2, seqs, 8, cols).transpose(0, 2, 1, 3).reshape(16, seqs * cols // 128, 128)
    got = lax.all_to_all(parts, "tp", 0, 0, tiled=True)
    mlp_out = jnp.sum(got, axis=0).reshape(seqs, cols).astype(BF16)
    return (
        jnp.concatenate(firsts, axis=1).T,
        jnp.concatenate(seconds, axis=1).T,
        weight,
        mlp_out,
    )


def solution(mesh):
    placed = (
        P("tp", ("learn", "dp")),
        P(("learn", "dp"), None),
        P("tp", ("learn", "dp")),
        P("tp", ("learn", "dp")),
        P(("learn", "dp")),
        P("tp", ("learn", "dp")),
        P("dp", "tp"),
    )
    return jax.shard_map(
        shards,
        mesh=mesh,
        in_specs=placed,
        out_specs=(
            P("tp", ("learn", "dp")),
            P("tp", ("learn", "dp")),
            P("tp", ("learn", "dp")),
            P("dp", ("learn", "tp")),
        ),
        check_vma=False,
    )
```

time: 345 us -> 144 us (0.42)
  waiting for transfers between devices: 308 us -> 33.7 us
  starting transfers between devices: 0.16 us -> 67 us
  Pallas kernels: 0 us -> 24.3 us
  matrix products: 16.2 us -> 0 us
  between operations: 13.8 us -> 1 us
  local copies, waits for them, and re-layouts: 4.52 us -> 11.9 us
    reduce_scatter x1 -> x0, waiting for transfers between devices: 135 us -> none  [shards(): lax.psum_scatter(partial_low, ('learn', 'dp'), scatter_dimension=1, tiled...]
    all_gather x2 -> x0, waiting for transfers between devices: 86.3 us -> none  [the longest x1 72 us: shards(): lax.all_gather(ratio, ('learn', 'dp'), axis=1, tiled=True)]
    unnamed x5 -> x0, waiting for transfers between devices: 86.3 us -> none
    ppermute x0 -> x35, starting transfers between devices: none -> 60.9 us  [the longest x4 26.6 us: shards(): far = lambda v: lax.ppermute(v, 'learn', across)]
    pallas_call x0 -> x5, Pallas kernels: none -> 24.3 us  [the longest x2 11.4 us: update(): pl.pallas_call(functools.partial(update_kernel, first, rows, weight is no...]
    ppermute x0 -> x35, waiting for transfers between devices: none -> 23.3 us  [the longest x12 12.9 us: shards(): minus = lambda v: lax.ppermute(v, 'learn', down)]
    dot_general x3 -> x0, matrix products: 16.2 us -> none  [the longest x1 6.67 us: shards(): lax.dot_general(lax.all_gather(ratio, ('learn', 'dp'), axis=1, tiled=True...]
    all_to_all x0 -> x1, waiting for transfers between devices: none -> 10.3 us  [shards(): got = lax.all_to_all(parts, 'tp', 0, 0, tiled=True)]
  transfers between devices with their start and end apart: 4 -> 36, of which waited for: 4 -> 14; matrix products, arithmetic and copies ran while one was open for 0% -> 7% of each run, Pallas kernels for 0% -> 9%
where the time goes in v1:
time: 144 us; the launch traced here: 143 us
  starting transfers between devices  67 us (47%)
  waiting for transfers between devices  33.7 us (23%)
  Pallas kernels  24.3 us (17%)
  local copies, waits for them, and re-layouts  11.9 us (8%)
  other arithmetic  5.72 us (4%)
    ppermute x4, starting transfers between devices, shards(): far = lambda v: lax.ppermute(v, 'learn', across)  26.6 us
    ppermute x12, starting transfers between devices, shards(): plus = lambda v: lax.ppermute(v, 'learn', up)  26.4 us
    ppermute x12, waiting for transfers between devices, shards(): minus = lambda v: lax.ppermute(v, 'learn', down)  12.9 us
    pallas_call x2, Pallas kernels, update(): pl.pallas_call(functools.partial(update_kernel, first, rows, weight is no...  11.4 us
    all_to_all x1, waiting for transfers between devices, shards(): got = lax.all_to_all(parts, 'tp', 0, 0, tiled=True)  10.3 us
    pallas_call x2, Pallas kernels, project(): pl.pallas_call(project_kernel, grid=(steps,), in_specs=[pl.BlockSpec((ran...  9.63 us
    all_to_all x1, starting transfers between devices, shards(): got = lax.all_to_all(parts, 'tp', 0, 0, tiled=True)  6.09 us
    ppermute x12, starting transfers between devices, shards(): minus = lambda v: lax.ppermute(v, 'learn', down)  5.93 us
  transfers between devices with their start and end apart: 36, of which 14 were waited for; matrix products, arithmetic and copies ran while one was open for 7% of the time, Pallas kernels for 9%

profile of v1, /device:TPU:6, one launch (start us, length us, event | category | flops | bytes accessed | tf_op | source)
XLA Modules:
  0.0 143.5 jit_solution(12182134855569152292)
XLA Ops:
  4.4 3.2 %shard_map.102 = (bf16[512,512]{1,0:T(8,128)(2,1)}, bf16[512,512]{1,0:T(8,128)(2,1)}) custom-call(s32[3]{0:T(128)} %pad_add_fusion.where_ref, bf16[512,1024]{1,0:T(8,128)(2,1)} %basis_ref.1), custom_call_target="tpu_custom_call" | custom-call | bytes 4194304 | tf_op jit(solution)/shard_map/pallas_call | solution.py:38
  10.6 4.8 %shard_map.104 = (f32[64,824]{1,0:T(8,128)}, f32[64,824]{1,0:T(8,128)}, f32[64,824]{1,0:T(8,128)}, f32[64,824]{1,0:T(8,128)}, f32[64,824]{1,0:T(8,128)}, /*index...) custom-call(bf16[512,512]{1,0:T(8,128)(2,1)} %get-tuple-element.26.own_ref.refs_2_.refs_3_, ...), custom_call_target="tpu_custom_call" | custom-call | flops 864026624 | bytes 3375104 | tf_op jit(solution)/shard_map/pallas_call | solution.py:66
  16.3 2.4 %collective-permute-start.10 = (f32[64,824]{1,0:T(8,128)}, f32[64,824]{1,0:T(8,128)S(1)}, u32[]{:S(2)}, u32[]{:S(2)}) collective-permute-start(f32[64,824]{1,0:T(8,128)} %get-tuple-element.38), channel_id=1, source_target_pairs={{0,32},{32,64},{64,96},{96,0},{128,160},{160,192},{192,224},{224,1... | collective-permute-start | bytes 632840 | tf_op jit(solution)/shard_map/ppermute | solution.py:154
  19.8 4.8 %collective-permute-done.14 = f32[64,824]{1,0:T(8,128)S(1)} collective-permute-done((f32[64,824]{1,0:T(8,128)}, f32[64,824]{1,0:T(8,128)S(1)}, u32[]{:S(2)}, u32[]{:S(2)}) %collective-permute-start.14) | collective-permute-done | bytes 210976 | tf_op jit(solution)/shard_map/ppermute | solution.py:155
  27.4 4.8 %shard_map.103 = (f32[64,1024]{1,0:T(8,128)}, f32[64,1024]{1,0:T(8,128)}, f32[64,1024]{1,0:T(8,128)}, f32[64,1024]{1,0:T(8,128)}, f32[64,1024]{1,0:T(8,128)}, /*...) custom-call(bf16[512,512]{1,0:T(8,128)(2,1)} %get-tuple-element.26.own_ref.refs_2_.refs_3_, ...), custom_call_target="tpu_custom_call" | custom-call | flops 1073741824 | bytes 4194304 | tf_op jit(solution)/shard_map/pallas_call | solution.py:66
  32.2 2.3 %collective-permute-start.6 = (f32[64,1024]{1,0:T(8,128)}, f32[64,1024]{1,0:T(8,128)S(1)}, u32[]{:S(2)}, u32[]{:S(2)}) collective-permute-start(f32[64,1024]{1,0:T(8,128)} %get-tuple-element.35), channel_id=1, source_target_pairs={{32,0},{64,32},{96,64},{0,96},{160,128},{192,160},{224,192},{128,2... | collective-permute-start | bytes 786440 | tf_op jit(solution)/shard_map/ppermute | solution.py:155
  37.7 7.3 %collective-permute-start.16 = (f32[64,824]{1,0:T(8,128)S(1)}, f32[64,824]{1,0:T(8,128)S(1)}, u32[]{:S(2)}, u32[]{:S(2)}) collective-permute-start(f32[64,824]{1,0:T(8,128)S(1)} %add_add_fusion.2), channel_id=1, source_target_pairs={{0,128},{32,160},{64,192},{96,224},{128,0},{160,32},{192,64},{224,... | collective-permute-start | bytes 632840 | tf_op jit(solution)/shard_map/ppermute | solution.py:156
  48.6 3.1 %collective-permute-start.3 = (f32[64,1024]{1,0:T(8,128)S(1)}, f32[64,1024]{1,0:T(8,128)S(1)}, u32[]{:S(2)}, u32[]{:S(2)}) collective-permute-start(f32[64,1024]{1,0:T(8,128)S(1)} %add.72), channel_id=1, source_target_pairs={{0,32},{32,64},{64,96},{96,0},{128,160},{160,192},{192,224},{224,1... | collective-permute-start | bytes 786440 | tf_op jit(solution)/shard_map/ppermute | solution.py:154
  53.7 6.4 %collective-permute-start.26 = (bf16[64,824]{1,0:T(8,128)(2,1)S(1)}, bf16[64,824]{1,0:T(8,128)(2,1)S(1)}, u32[]{:S(2)}, u32[]{:S(2)}) collective-permute-start(bf16[64,824]{1,0:T(8,128)(2,1)S(1)} %get-tuple-element.49), channel_id=1, source_target_pairs={{0,128},{32,160},{64,192},{96,224},{128,0},{160,32},{192,64},{224,... | collective-permute-start | bytes 316424 | tf_op jit(solution)/shard_map/ppermute | solution.py:156
  60.5 2.9 %collective-permute-start.29 = (bf16[64,824]{1,0:T(8,128)(2,1)S(1)}, bf16[64,824]{1,0:T(8,128)(2,1)S(1)}, u32[]{:S(2)}, u32[]{:S(2)}) collective-permute-start(bf16[64,824]{1,0:T(8,128)(2,1)S(1)} %get-tuple-element.49), channel_id=1, source_target_pairs={{0,32},{32,64},{64,96},{96,0},{128,160},{160,192},{192,224},{224,1... | collective-permute-start | bytes 316424 | tf_op jit(solution)/shard_map/ppermute | solution.py:154
  63.6 6.4 %collective-permute-start.8 = (f32[64,1024]{1,0:T(8,128)S(1)}, f32[64,1024]{1,0:T(8,128)S(1)}, u32[]{:S(2)}, u32[]{:S(2)}) collective-permute-start(f32[64,1024]{1,0:T(8,128)S(1)} %add_add_fusion), channel_id=1, source_target_pairs={{0,128},{32,160},{64,192},{96,224},{128,0},{160,32},{192,64},{224,... | collective-permute-start | bytes 786440 | tf_op jit(solution)/shard_map/ppermute | solution.py:156
  70.3 3.2 %collective-permute-start.32 = (bf16[64,824]{1,0:T(8,128)(2,1)S(1)}, bf16[64,824]{1,0:T(8,128)(2,1)S(1)}, u32[]{:S(2)}, u32[]{:S(2)}) collective-permute-start(bf16[64,824]{1,0:T(8,128)(2,1)S(1)} %collective-permute-done.26), channel_id=1, source_target_pairs={{0,32},{32,64},{64,96},{96,0},{128,160},{160,192},{192,224},{224,1... | collective-permute-start | bytes 316424 | tf_op jit(solution)/shard_map/ppermute | solution.py:154
  73.4 2.7 %collective-permute-done.28 = bf16[64,824]{1,0:T(8,128)(2,1)S(1)} collective-permute-done((bf16[64,824]{1,0:T(8,128)(2,1)S(1)}, bf16[64,824]{1,0:T(8,128)(2,1)S(1)}, u32[]{:S(2)}, u32[]{:S(2)}) %collective-permute-start.28) | collective-permute-done | bytes 105504 | tf_op jit(solution)/shard_map/ppermute | solution.py:155
  79.2 6.6 %collective-permute-start.17 = (bf16[64,1024]{1,0:T(8,128)(2,1)S(1)}, bf16[64,1024]{1,0:T(8,128)(2,1)S(1)}, u32[]{:S(2)}, u32[]{:S(2)}) collective-permute-start(bf16[64,1024]{1,0:T(8,128)(2,1)S(1)} %get-tuple-element.53), channel_id=1, source_target_pairs={{0,128},{32,160},{64,192},{96,224},{128,0},{160,32},{192,64},{224,... | collective-permute-start | bytes 393224 | tf_op jit(solution)/shard_map/ppermute | solution.py:156
  85.9 3.2 %collective-permute-start.20 = (bf16[64,1024]{1,0:T(8,128)(2,1)S(1)}, bf16[64,1024]{1,0:T(8,128)(2,1)S(1)}, u32[]{:S(2)}, u32[]{:S(2)}) collective-permute-start(bf16[64,1024]{1,0:T(8,128)(2,1)S(1)} %get-tuple-element.53), channel_id=1, source_target_pairs={{0,32},{32,64},{64,96},{96,0},{128,160},{160,192},{192,224},{224,1... | collective-permute-start | bytes 393224 | tf_op jit(solution)/shard_map/ppermute | solution.py:154
  90.2 3.2 %collective-permute-start.23 = (bf16[64,1024]{1,0:T(8,128)(2,1)S(1)}, bf16[64,1024]{1,0:T(8,128)(2,1)S(1)}, u32[]{:S(2)}, u32[]{:S(2)}) collective-permute-start(bf16[64,1024]{1,0:T(8,128)(2,1)S(1)} %collective-permute-done.17), channel_id=1, source_target_pairs={{0,32},{32,64},{64,96},{96,0},{128,160},{160,192},{192,224},{224,1... | collective-permute-start | bytes 393224 | tf_op jit(solution)/shard_map/ppermute | solution.py:154
  96.4 2.1 %collective-permute-done.21 = bf16[64,1024]{1,0:T(8,128)(2,1)S(1)} collective-permute-done((bf16[64,1024]{1,0:T(8,128)(2,1)S(1)}, bf16[64,1024]{1,0:T(8,128)(2,1)S(1)}, u32[]{:S(2)}, u32[]{:S(2)}) %collective-permute-start.21) | collective-permute-done | bytes 131104 | tf_op jit(solution)/shard_map/ppermute | solution.py:154
  98.5 4.0 %collective-permute-done.22 = bf16[64,1024]{1,0:T(8,128)(2,1)S(1)} collective-permute-done((bf16[64,1024]{1,0:T(8,128)(2,1)S(1)}, bf16[64,1024]{1,0:T(8,128)(2,1)S(1)}, u32[]{:S(2)}, u32[]{:S(2)}) %collective-permute-start.22) | collective-permute-done | bytes 131104 | tf_op jit(solution)/shard_map/ppermute | solution.py:155
  104.8 2.4 %collective-permute-done.33 = bf16[512,824]{0,1:T(8,128)(2,1)} collective-permute-done((bf16[512,824]{0,1:T(8,128)(2,1)}, bf16[512,824]{0,1:T(8,128)(2,1)}, u32[]{:S(2)}, u32[]{:S(2)}) %collective-permute-start.33) | collective-permute-done | bytes 843808 | tf_op jit(solution)/shard_map/ppermute | solution.py:157
  107.1 2.2 %copy.17.refs_2_ = bf16[512,824]{1,0:T(8,128)(2,1)} copy(bf16[512,824]{0,1:T(8,128)(2,1)} %collective-permute-done.33) | data formatting | bytes 1687552 | tf_op jit(solution)/shard_map/ppermute | solution.py:157
  110.4 5.8 %shard_map.105 = (bf16[1848,512]{1,0:T(8,128)(2,1)}, f32[128,512]{1,0:T(8,128)}) custom-call(bf16[512,1024]{1,0:T(8,128)(2,1)} %copy-done.2, bf16[512,1024]{1,0:T(8,128)(2,1)} %copy-done.4, bf16[512,512]{1,0:T(8,128)(2,1)} %get-tuple-element.26.own_ref.refs_2_.refs_3_, bf16[512,512]{1,0:T(8,128)(2,1)} %get-tuple-element.27.refs_3_.refs_4_, ...), custom_call_target="tpu_custom_call" | custom-call | flops 1073741824 | bytes 4194304 | tf_op jit(solution)/shard_map/pallas_call | solution.py:129
  116.2 5.7 %shard_map.106 = (bf16[1848,512]{1,0:T(8,128)(2,1)}, f32[128,512]{1,0:T(8,128)}) custom-call(bf16[1848,512]{1,0:T(8,128)(2,1)} %get-tuple-element.44.refs_0_, bf16[512,824]{1,0:T(8,128)(2,1)} %copy-done, bf16[512,824]{1,0:T(8,128)(2,1)} %copy.17.refs_2_, bf16[512,512]{1,0:T(8,128)(2,1)} %get-tuple-element.26.own_ref.refs_2_.refs_3_, ...), custom_call_target="tpu_custom_call", output_to_operand_aliasing={{0}: (0, {})} | custom-call | flops 864026624 | bytes 3375104 | tf_op jit(solution)/shard_map/pallas_call | solution.py:129
  125.3 6.1 %all-to-all-start = ((f32[16,32,128]{2,1,0:T(8,128)}), f32[16,32,128]{2,1,0:T(8,128)S(1)}, u32[]{:S(2)}, u32[]{:S(2)}) async-start(f32[16,32,128]{2,1,0:T(8,128)} %reshape.23), calls=%async_computation | async-start | bytes 524288 | tf_op jit(solution)/shard_map/all_to_all | solution.py:214
  132.4 10.3 %all-to-all-done = f32[16,32,128]{2,1,0:T(8,128)S(1)} async-done(((f32[16,32,128]{2,1,0:T(8,128)}), f32[16,32,128]{2,1,0:T(8,128)S(1)}, u32[]{:S(2)}, u32[]{:S(2)}) %all-to-all-start) | async-done | bytes 262176 | tf_op jit(solution)/shard_map/all_to_all | solution.py:214
  (126 shorter events, 36.5 us)
Async XLA Ops:
  3.2 23.2 %collective-permute-start.1 = (bf16[1024,512]{1,0:T(8,128)(2,1)S(1)}, bf16[1024,512]{1,0:T(8,128)(2,1)S(1)}, u32[]{:S(2)}, u32[]{:S(2)}) collective-permute-start(bf16[1024,512]{1,0:T(8,128)(2,1)S(1)} %slice.25), channel_id=1, source_target_pairs={{0,1},{1,0},{2,3},{3,2},{4,5},{5,4},{6,7},{7,6},{8,9},{9,8},{10,11... | collective-permute-start | bytes 3145736 | tf_op jit(solution)/shard_map/ppermute | solution.py:157
  16.3 18.2 %collective-permute-start.10 = (f32[64,824]{1,0:T(8,128)}, f32[64,824]{1,0:T(8,128)S(1)}, u32[]{:S(2)}, u32[]{:S(2)}) collective-permute-start(f32[64,824]{1,0:T(8,128)} %get-tuple-element.38), channel_id=1, source_target_pairs={{0,32},{32,64},{64,96},{96,0},{128,160},{160,192},{192,224},{224,1... | collective-permute-start | bytes 632840 | tf_op jit(solution)/shard_map/ppermute | solution.py:154
  18.8 16.8 %collective-permute-start.13 = (f32[64,824]{1,0:T(8,128)}, f32[64,824]{1,0:T(8,128)S(1)}, u32[]{:S(2)}, u32[]{:S(2)}) collective-permute-start(f32[64,824]{1,0:T(8,128)} %get-tuple-element.41), channel_id=1, source_target_pairs={{0,32},{32,64},{64,96},{96,0},{128,160},{160,192},{192,224},{224,1... | collective-permute-start | bytes 632840 | tf_op jit(solution)/shard_map/ppermute | solution.py:154
  26.2 11.4 %collective-permute-start.15 = (f32[64,824]{1,0:T(8,128)}, f32[64,824]{1,0:T(8,128)S(1)}, u32[]{:S(2)}, u32[]{:S(2)}) collective-permute-start(f32[64,824]{1,0:T(8,128)} %add.84), channel_id=1, source_target_pairs={{32,0},{64,32},{96,64},{0,96},{160,128},{192,160},{224,192},{128,2... | collective-permute-start | bytes 632840 | tf_op jit(solution)/shard_map/ppermute | solution.py:155
  26.3 21.9 %collective-permute-start.12 = (f32[64,824]{1,0:T(8,128)}, f32[64,824]{1,0:T(8,128)S(1)}, u32[]{:S(2)}, u32[]{:S(2)}) collective-permute-start(f32[64,824]{1,0:T(8,128)} %get-tuple-element.39), channel_id=1, source_target_pairs={{32,0},{64,32},{96,64},{0,96},{160,128},{192,160},{224,192},{128,2... | collective-permute-start | bytes 632840 | tf_op jit(solution)/shard_map/ppermute | solution.py:155
  32.2 12.8 %collective-permute-start.6 = (f32[64,1024]{1,0:T(8,128)}, f32[64,1024]{1,0:T(8,128)S(1)}, u32[]{:S(2)}, u32[]{:S(2)}) collective-permute-start(f32[64,1024]{1,0:T(8,128)} %get-tuple-element.35), channel_id=1, source_target_pairs={{32,0},{64,32},{96,64},{0,96},{160,128},{192,160},{224,192},{128,2... | collective-permute-start | bytes 786440 | tf_op jit(solution)/shard_map/ppermute | solution.py:155
  34.6 13.4 %collective-permute-start.2 = (f32[64,1024]{1,0:T(8,128)}, f32[64,1024]{1,0:T(8,128)S(1)}, u32[]{:S(2)}, u32[]{:S(2)}) collective-permute-start(f32[64,1024]{1,0:T(8,128)} %get-tuple-element.30), channel_id=1, source_target_pairs={{0,32},{32,64},{64,96},{96,0},{128,160},{160,192},{192,224},{224,1... | collective-permute-start | bytes 786440 | tf_op jit(solution)/shard_map/ppermute | solution.py:154
  35.6 13.0 %collective-permute-start.11 = (f32[64,824]{1,0:T(8,128)S(1)}, f32[64,824]{1,0:T(8,128)S(1)}, u32[]{:S(2)}, u32[]{:S(2)}) collective-permute-start(f32[64,824]{1,0:T(8,128)S(1)} %add.80), channel_id=1, source_target_pairs={{0,32},{32,64},{64,96},{96,0},{128,160},{160,192},{192,224},{224,1... | collective-permute-start | bytes 632840 | tf_op jit(solution)/shard_map/ppermute | solution.py:154
  37.7 15.0 %collective-permute-start.16 = (f32[64,824]{1,0:T(8,128)S(1)}, f32[64,824]{1,0:T(8,128)S(1)}, u32[]{:S(2)}, u32[]{:S(2)}) collective-permute-start(f32[64,824]{1,0:T(8,128)S(1)} %add_add_fusion.2), channel_id=1, source_target_pairs={{0,128},{32,160},{64,192},{96,224},{128,0},{160,32},{192,64},{224,... | collective-permute-start | bytes 632840 | tf_op jit(solution)/shard_map/ppermute | solution.py:156
  45.0 15.1 %collective-permute-start.5 = (f32[64,1024]{1,0:T(8,128)}, f32[64,1024]{1,0:T(8,128)S(1)}, u32[]{:S(2)}, u32[]{:S(2)}) collective-permute-start(f32[64,1024]{1,0:T(8,128)} %get-tuple-element.33), channel_id=1, source_target_pairs={{0,32},{32,64},{64,96},{96,0},{128,160},{160,192},{192,224},{224,1... | collective-permute-start | bytes 786440 | tf_op jit(solution)/shard_map/ppermute | solution.py:154
  48.0 28.6 %collective-permute-start.4 = (f32[64,1024]{1,0:T(8,128)S(1)}, f32[64,1024]{1,0:T(8,128)S(1)}, u32[]{:S(2)}, u32[]{:S(2)}) collective-permute-start(f32[64,1024]{1,0:T(8,128)S(1)} %copy-done.15), channel_id=1, source_target_pairs={{32,0},{64,32},{96,64},{0,96},{160,128},{192,160},{224,192},{128,2... | collective-permute-start | bytes 786440 | tf_op jit(solution)/shard_map/ppermute | solution.py:155
  48.2 12.2 %collective-permute-start.7 = (f32[64,1024]{1,0:T(8,128)S(1)}, f32[64,1024]{1,0:T(8,128)S(1)}, u32[]{:S(2)}, u32[]{:S(2)}) collective-permute-start(f32[64,1024]{1,0:T(8,128)S(1)} %add.76), channel_id=1, source_target_pairs={{32,0},{64,32},{96,64},{0,96},{160,128},{192,160},{224,192},{128,2... | collective-permute-start | bytes 786440 | tf_op jit(solution)/shard_map/ppermute | solution.py:155
  48.6 29.7 %collective-permute-start.3 = (f32[64,1024]{1,0:T(8,128)S(1)}, f32[64,1024]{1,0:T(8,128)S(1)}, u32[]{:S(2)}, u32[]{:S(2)}) collective-permute-start(f32[64,1024]{1,0:T(8,128)S(1)} %add.72), channel_id=1, source_target_pairs={{0,32},{32,64},{64,96},{96,0},{128,160},{160,192},{192,224},{224,1... | collective-permute-start | bytes 786440 | tf_op jit(solution)/shard_map/ppermute | solution.py:154
  53.7 9.9 %collective-permute-start.26 = (bf16[64,824]{1,0:T(8,128)(2,1)S(1)}, bf16[64,824]{1,0:T(8,128)(2,1)S(1)}, u32[]{:S(2)}, u32[]{:S(2)}) collective-permute-start(bf16[64,824]{1,0:T(8,128)(2,1)S(1)} %get-tuple-element.49), channel_id=1, source_target_pairs={{0,128},{32,160},{64,192},{96,224},{128,0},{160,32},{192,64},{224,... | collective-permute-start | bytes 316424 | tf_op jit(solution)/shard_map/ppermute | solution.py:156
  60.1 9.9 %collective-permute-start.27 = (bf16[64,824]{1,0:T(8,128)(2,1)S(1)}, bf16[64,824]{1,0:T(8,128)(2,1)S(1)}, u32[]{:S(2)}, u32[]{:S(2)}) collective-permute-start(bf16[64,824]{1,0:T(8,128)(2,1)S(1)} %get-tuple-element.49), channel_id=1, source_target_pairs={{32,0},{64,32},{96,64},{0,96},{160,128},{192,160},{224,192},{128,2... | collective-permute-start | bytes 316424 | tf_op jit(solution)/shard_map/ppermute | solution.py:155
  60.5 9.8 %collective-permute-start.29 = (bf16[64,824]{1,0:T(8,128)(2,1)S(1)}, bf16[64,824]{1,0:T(8,128)(2,1)S(1)}, u32[]{:S(2)}, u32[]{:S(2)}) collective-permute-start(bf16[64,824]{1,0:T(8,128)(2,1)S(1)} %get-tuple-element.49), channel_id=1, source_target_pairs={{0,32},{32,64},{64,96},{96,0},{128,160},{160,192},{192,224},{224,1... | collective-permute-start | bytes 316424 | tf_op jit(solution)/shard_map/ppermute | solution.py:154
  63.6 15.3 %collective-permute-start.8 = (f32[64,1024]{1,0:T(8,128)S(1)}, f32[64,1024]{1,0:T(8,128)S(1)}, u32[]{:S(2)}, u32[]{:S(2)}) collective-permute-start(f32[64,1024]{1,0:T(8,128)S(1)} %add_add_fusion), channel_id=1, source_target_pairs={{0,128},{32,160},{64,192},{96,224},{128,0},{160,32},{192,64},{224,... | collective-permute-start | bytes 786440 | tf_op jit(solution)/shard_map/ppermute | solution.py:156
  70.3 32.7 %collective-permute-start.32 = (bf16[64,824]{1,0:T(8,128)(2,1)S(1)}, bf16[64,824]{1,0:T(8,128)(2,1)S(1)}, u32[]{:S(2)}, u32[]{:S(2)}) collective-permute-start(bf16[64,824]{1,0:T(8,128)(2,1)S(1)} %collective-permute-done.26), channel_id=1, source_target_pairs={{0,32},{32,64},{64,96},{96,0},{128,160},{160,192},{192,224},{224,1... | collective-permute-start | bytes 316424 | tf_op jit(solution)/shard_map/ppermute | solution.py:154
  76.1 9.7 %collective-permute-start.30 = (bf16[64,824]{1,0:T(8,128)(2,1)S(1)}, bf16[64,824]{1,0:T(8,128)(2,1)S(1)}, u32[]{:S(2)}, u32[]{:S(2)}) collective-permute-start(bf16[64,824]{1,0:T(8,128)(2,1)S(1)} %collective-permute-done.29), channel_id=1, source_target_pairs={{0,32},{32,64},{64,96},{96,0},{128,160},{160,192},{192,224},{224,1... | collective-permute-start | bytes 316424 | tf_op jit(solution)/shard_map/ppermute | solution.py:154
  76.6 12.5 %collective-permute-start.31 = (bf16[64,824]{1,0:T(8,128)(2,1)S(1)}, bf16[64,824]{1,0:T(8,128)(2,1)S(1)}, u32[]{:S(2)}, u32[]{:S(2)}) collective-permute-start(bf16[64,824]{1,0:T(8,128)(2,1)S(1)} %collective-permute-done.28), channel_id=1, source_target_pairs={{32,0},{64,32},{96,64},{0,96},{160,128},{192,160},{224,192},{128,2... | collective-permute-start | bytes 316424 | tf_op jit(solution)/shard_map/ppermute | solution.py:155
  79.2 11.0 %collective-permute-start.17 = (bf16[64,1024]{1,0:T(8,128)(2,1)S(1)}, bf16[64,1024]{1,0:T(8,128)(2,1)S(1)}, u32[]{:S(2)}, u32[]{:S(2)}) collective-permute-start(bf16[64,1024]{1,0:T(8,128)(2,1)S(1)} %get-tuple-element.53), channel_id=1, source_target_pairs={{0,128},{32,160},{64,192},{96,224},{128,0},{160,32},{192,64},{224,... | collective-permute-start | bytes 393224 | tf_op jit(solution)/shard_map/ppermute | solution.py:156
  85.8 9.5 %collective-permute-start.18 = (bf16[64,1024]{1,0:T(8,128)(2,1)S(1)}, bf16[64,1024]{1,0:T(8,128)(2,1)S(1)}, u32[]{:S(2)}, u32[]{:S(2)}) collective-permute-start(bf16[64,1024]{1,0:T(8,128)(2,1)S(1)} %get-tuple-element.53), channel_id=1, source_target_pairs={{32,0},{64,32},{96,64},{0,96},{160,128},{192,160},{224,192},{128,2... | collective-permute-start | bytes 393224 | tf_op jit(solution)/shard_map/ppermute | solution.py:155
  90.2 12.4 %collective-permute-start.23 = (bf16[64,1024]{1,0:T(8,128)(2,1)S(1)}, bf16[64,1024]{1,0:T(8,128)(2,1)S(1)}, u32[]{:S(2)}, u32[]{:S(2)}) collective-permute-start(bf16[64,1024]{1,0:T(8,128)(2,1)S(1)} %collective-permute-done.17), channel_id=1, source_target_pairs={{0,32},{32,64},{64,96},{96,0},{128,160},{160,192},{192,224},{224,1... | collective-permute-start | bytes 393224 | tf_op jit(solution)/shard_map/ppermute | solution.py:154
  125.3 17.5 %all-to-all-start = ((f32[16,32,128]{2,1,0:T(8,128)}), f32[16,32,128]{2,1,0:T(8,128)S(1)}, u32[]{:S(2)}, u32[]{:S(2)}) async-start(f32[16,32,128]{2,1,0:T(8,128)} %reshape.23), calls=%async_computation | async-start | bytes 524288 | tf_op jit(solution)/shard_map/all_to_all | solution.py:214
  (29 other events, 283.5 us)

commit v2 on v0

v2 whole, which is shorter than its diff:
```python
import functools

import jax
import jax.numpy as jnp
from jax import lax
from jax.experimental import pallas as pl
from jax.experimental.pallas import tpu as pltpu
from jax.sharding import PartitionSpec as P

BETA_ONE = 0.9
BETA_TWO = 0.999
ADAM_EPS = 1e-06
STEP_RATE = 0.01
RING = 4
ROWS = 384
VMEM = 16 * 2**20
F32 = jnp.float32
BF16 = jnp.bfloat16
SHAPE = jax.ShapeDtypeStruct
ORDER = (0, 1, 3, 2)


WHOLE = pl.BlockSpec(memory_space=pltpu.VMEM)
ANYWHERE = pl.BlockSpec(memory_space=pl.ANY)


def call(kernel, out_shape, args, in_specs=None, out_specs=None, grid=(), deps=(), held=(), scratch=()):
    n_in, n_out, n_held = len(args), len(out_shape), len(held)

    def body(*refs):
        rest = refs[n_in + n_held + len(deps) :]
        kernel(*refs[:n_in], *rest[:n_out], *rest[n_out + n_held :])

    specs = list(in_specs or [WHOLE] * n_in)
    args = [pltpu.with_memory_space_constraint(a, pltpu.VMEM) if s is WHOLE else a for a, s in zip(args, specs)]
    out_specs = list(out_specs or [WHOLE] * n_out)
    out_shape = [pltpu.VMEM(o.shape, o.dtype) if s is WHOLE else o for o, s in zip(out_shape, out_specs)]

    return pl.pallas_call(
        body,
        grid=grid,
        in_specs=specs + [ANYWHERE] * (n_held + len(deps)),
        out_specs=out_specs + [ANYWHERE] * n_held,
        out_shape=list(out_shape) + [SHAPE(h.shape, h.dtype) for h in held],
        scratch_shapes=list(scratch),
        input_output_aliases={n_in + i: n_out + i for i in range(n_held)},
        compiler_params=pltpu.CompilerParams(vmem_limit_bytes=VMEM),
        cost_estimate=pl.CostEstimate(flops=0, bytes_accessed=0, transcendentals=0),
    )(*args, *held, *deps)


def arrange_kernel(where_ref, basis_ref, all_ref, send_ref, turned):
    zh, x, d = where_ref[0], where_ref[1], where_ref[2]
    width = turned.shape[0] // 16
    turned[...] = basis_ref[...].T
    for side in range(2):
        for place, j in enumerate(ORDER):
            for zrel in range(2):
                block = ((zh ^ zrel) * RING + ((x + j) & (RING - 1))) * 2 + (d ^ side)
                rows = turned[pl.ds(pl.multiple_of(block * width, width), width), :]
                first = (RING * zrel + place) * width
                if side == 1:
                    send_ref[first : first + width, :] = rows
                first += side * 8 * width
                all_ref[first : first + width, :] = rows


def arrange(where, basis):
    depth, rank = basis.shape
    return pl.pallas_call(
        arrange_kernel,
        grid_spec=pltpu.PrefetchScalarGridSpec(
            num_scalar_prefetch=1,
            grid=(1,),
            in_specs=[pl.BlockSpec((depth, rank), lambda i, w: (0, 0))],
            out_specs=[
                pl.BlockSpec((rank, depth), lambda i, w: (0, 0)),
                pl.BlockSpec((rank // 2, depth), lambda i, w: (0, 0)),
            ],
            scratch_shapes=[pltpu.VMEM((rank, depth), basis.dtype)],
        ),
        out_shape=(SHAPE((rank, depth), basis.dtype), SHAPE((rank // 2, depth), basis.dtype)),
        compiler_params=pltpu.CompilerParams(vmem_limit_bytes=VMEM),
        cost_estimate=pl.CostEstimate(flops=0, bytes_accessed=0, transcendentals=0),
    )(where, basis)


def chunks(rows):
    return [(at, min(ROWS, rows - at)) for at in range(0, rows, ROWS)]


def project_kernel(zrel, own_ref, other_ref, mine_ref, theirs_ref, up_out, down_out, up2_out, down2_out, own_out):
    contract = (((1,), (1,)), ((), ()))
    w = own_out.shape[0]
    h = w // 2
    ranks = slice(zrel * RING * w, (zrel + 1) * RING * w)
    for at, n in chunks(mine_ref.shape[0]):
        rows = slice(at, at + n)
        low = lax.dot_general(own_ref[ranks, :], mine_ref[rows, :], contract, preferred_element_type=F32)
        low += lax.dot_general(other_ref[ranks, :], theirs_ref[rows, :], contract, preferred_element_type=F32)
        own, above, below, two = (low[w * k : w * (k + 1)] for k in range(RING))
        up_out[:h, rows] = two[:h]
        up_out[h:, rows] = above[h:]
        down_out[:h, rows] = two[h:]
        down_out[h:, rows] = below[:h]
        up2_out[:, rows] = above[:h]
        down2_out[:, rows] = below[h:]
        own_out[:, rows] = own


def project(basis_all, basis_recv, gradient, theirs, zrel, count, deps=()):
    w = basis_recv.shape[0] // 8
    heights = (w, w, w // 2, w // 2, w)
    return call(
        functools.partial(project_kernel, zrel),
        [SHAPE((h, count), F32) for h in heights],
        (basis_all, basis_recv, gradient, theirs),
        deps=deps,
    )


def hop_kernel(up_ref, down_ref, below_ref, above_ref, up_out, down_out):
    h = up_ref.shape[0]
    up_out[...] = up_ref[...] + below_ref[:h, :]
    down_out[...] = down_ref[...] + above_ref[:h, :]


def hop(low, below, above, deps=()):
    shape = SHAPE(low[2].shape, F32)
    return call(hop_kernel, [shape, shape], (low[2], low[3], below, above), deps=deps)


def settle_kernel(own_ref, below_ref, above_ref, below2_ref, above2_ref, out_ref):
    h = below2_ref.shape[0]
    out_ref[:h, :] = own_ref[:h, :] + above_ref[h:, :] + below2_ref[...]
    out_ref[h:, :] = own_ref[h:, :] + below_ref[h:, :] + above2_ref[...]


def settle(low, first, second, held=()):
    return call(settle_kernel, [SHAPE(low[4].shape, F32)], (low[4], *first, *second), held=held)


def moment_step(sum_ref, came_ref, fresh_ref, first_ref, second_ref):
    here = slice(0, first_ref.shape[1])
    projected = sum_ref[:, here] + came_ref[:, here]
    fresh = fresh_ref[...] == 1
    start_first = jnp.where(fresh, F32(0.0), first_ref[...])
    start_second = jnp.where(fresh, F32(0.0), second_ref[...])
    new_first = BETA_ONE * start_first + (1.0 - BETA_ONE) * projected
    new_second = BETA_TWO * start_second + (1.0 - BETA_TWO) * projected * projected
    return new_first, new_second


def ratio_kernel(*refs):
    new_first, new_second = moment_step(*refs[:-1])
    refs[-1][:, : new_first.shape[1]] = (new_first / (jnp.sqrt(new_second) + ADAM_EPS)).astype(BF16)


def moments_kernel(*refs):
    refs[-2][...], refs[-1][...] = moment_step(*refs[:-2])


def hold(values, *deps):
    return call(lambda *refs: None, [], (), held=values, deps=deps)


def update_kernel(parts, *refs):
    basis_ref, old_ref, hid_ref, hid_far_ref, new_ref, out_ref, ratio = refs[parts:]
    at = 0
    for ref in refs[:parts]:
        ratio[at : at + ref.shape[0], :] = ref[...]
        at += ref.shape[0]
    contract = (((0,), (0,)), ((), ()))
    for at, n in chunks(old_ref.shape[0]):
        rows = slice(at, at + n)
        delta = lax.dot_general(ratio[:, rows], basis_ref[...], contract, preferred_element_type=F32)
        new = (old_ref[rows, :].astype(F32) - STEP_RATE * delta).astype(BF16)
        new_ref[rows, :] = new
        hid = jnp.concatenate([hid_ref[:, rows], hid_far_ref[:, rows]], axis=0)
        term = jnp.dot(hid, new, preferred_element_type=F32)
        if at == 0:
            out_ref[...] = term
        else:
            out_ref[...] += term


def update(ratios, basis_all, old, hid, hid_far):
    ranks, depth = basis_all.shape
    return call(
        functools.partial(update_kernel, len(ratios)),
        [SHAPE(old.shape, BF16), SHAPE((2 * hid.shape[0], depth), F32)],
        (*ratios, basis_all, old, hid, hid_far),
        scratch=[pltpu.VMEM((ranks, ratios[0].shape[1]), BF16)],
    )


def shards(gradient, frame_basis, moment_first, moment_second, refresh, old_weight, hidden):
    learn = lax.axis_index("learn")
    where = jnp.stack([learn // RING, learn % RING, lax.axis_index("dp")]).astype(jnp.int32)
    up = [(z * RING + x, z * RING + (x + 1) % RING) for z in range(2) for x in range(RING)]
    down = [(b, a) for a, b in up]
    across = [(i, (i + RING) % (2 * RING)) for i in range(2 * RING)]
    twice = [(z * RING + x, z * RING + (x + 2) % RING) for z in range(2) for x in range(RING)]
    plus = lambda v: lax.ppermute(v, "learn", up)
    minus = lambda v: lax.ppermute(v, "learn", down)
    far = lambda v: lax.ppermute(v, "learn", across)
    two_away = lambda v: lax.ppermute(v, "learn", twice)
    twin = lambda v: lax.ppermute(v, "dp", [(0, 1), (1, 0)])

    rows, depth = gradient.shape
    count = -(-rows // 128) * 128

    theirs = twin(gradient)
    basis_all, basis_send = arrange(where, frame_basis)
    basis_recv = twin(basis_send)
    hid_far = twin(hidden)
    fresh = refresh[:, None]

    give = project(basis_all, basis_recv, gradient, theirs, 1, count)
    give_got = plus(give[0]), minus(give[1])
    keep = project(basis_all, basis_recv, gradient, theirs, 0, count, deps=(give[0],))
    give_send = hop(give, *give_got, deps=(keep[0],))
    give_got2 = plus(give_send[0]), minus(give_send[1])
    given, *keep_held = settle(give, give_got, give_got2, keep[:2])
    came = far(given)
    keep_got = plus(keep_held[0]), minus(keep_held[1])
    keep_send = hop(keep, *keep_got)
    keep_got2 = plus(keep_send[0]), minus(keep_send[1])
    kept = settle(keep, keep_got, keep_got2)[0]
    args = (kept, came, fresh, moment_first.T, moment_second.T)
    r = call(ratio_kernel, [SHAPE(kept.shape, BF16)], args)[0]

    rz = far(r)
    below, above, opposite = plus(r), minus(r), two_away(r)
    new_first, new_second = call(moments_kernel, [SHAPE(moment_first.T.shape, F32)] * 2, args, deps=(r,))
    (rz,) = hold((rz,), below, above, opposite, hid_far, new_first)
    below_z, above_z = plus(rz), minus(rz)
    ratios = (r, above, below, opposite, rz, above_z, below_z, two_away(rz))
    others = [twin(v) for v in ratios]
    weight, total = update((*ratios, *others), basis_all, old_weight, hidden, hid_far)

    seqs = hidden.shape[0]
    here, there = total[:seqs], twin(total[seqs:])
    d = lax.axis_index("dp")
    pair = jnp.where(d == 0, jnp.stack([here, there]), jnp.stack([there, here]))
    cols = depth // 8
    parts = pair.reshape(2, seqs, 8, cols).transpose(0, 2, 1, 3).reshape(16, seqs * cols // 128, 128)
    got = lax.all_to_all(parts.astype(BF16), "tp", 0, 0, tiled=True)
    mlp_out = jnp.sum(got.astype(F32), axis=0).reshape(seqs, cols).astype(BF16)
    return new_first.T, new_second.T, weight, mlp_out


def solution(mesh):
    placed = (
        P("tp", ("learn", "dp")),
        P(("learn", "dp"), None),
        P("tp", ("learn", "dp")),
        P("tp", ("learn", "dp")),
        P(("learn", "dp")),
        P("tp", ("learn", "dp")),
        P("dp", "tp"),
    )
    return jax.shard_map(
        shards,
        mesh=mesh,
        in_specs=placed,
        out_specs=(
            P("tp", ("learn", "dp")),
            P("tp", ("learn", "dp")),
            P("tp", ("learn", "dp")),
            P("dp", ("learn", "tp")),
        ),
        check_vma=False,
    )
```

time: 345 us -> 118 us (0.34)
  waiting for transfers between devices: 308 us -> 47.4 us
  starting transfers between devices: 0.16 us -> 43.2 us
  matrix products: 16.2 us -> 0 us
  between operations: 13.8 us -> 0.88 us
  Pallas kernels: 0 us -> 10.7 us
  local copies, waits for them, and re-layouts: 4.52 us -> 13.5 us
    reduce_scatter x1 -> x0, waiting for transfers between devices: 135 us -> none  [shards(): lax.psum_scatter(partial_low, ('learn', 'dp'), scatter_dimension=1, tiled...]
    all_gather x2 -> x0, waiting for transfers between devices: 86.3 us -> none  [the longest x1 72 us: shards(): lax.all_gather(ratio, ('learn', 'dp'), axis=1, tiled=True)]
    unnamed x5 -> x0, waiting for transfers between devices: 86.3 us -> none
    ppermute x0 -> x28, waiting for transfers between devices: none -> 41.7 us  [the longest x6 15.8 us: shards(): minus = lambda v: lax.ppermute(v, 'learn', down)]
    ppermute x0 -> x28, starting transfers between devices: none -> 35.6 us  [the longest x2 15.7 us: shards(): far = lambda v: lax.ppermute(v, 'learn', across)]
    dot_general x3 -> x0, matrix products: 16.2 us -> none  [the longest x1 6.67 us: shards(): lax.dot_general(lax.all_gather(ratio, ('learn', 'dp'), axis=1, tiled=True...]
    pallas_call x0 -> x11, Pallas kernels: none -> 10.7 us  [the longest x10 9.79 us: call(): pl.pallas_call(body, grid=grid, in_specs=specs + [ANYWHERE] * (n_held + l...]
    all_to_all x0 -> x1, starting transfers between devices: none -> 7.62 us  [shards(): got = lax.all_to_all(parts.astype(BF16), 'tp', 0, 0, tiled=True)]
  transfers between devices with their start and end apart: 4 -> 29, of which waited for: 4 -> 17; matrix products, arithmetic and copies ran while one was open for 0% -> 3% of each run, Pallas kernels for 0% -> 4%
where the time goes in v2:
time: 118 us; the launch traced here: 116 us
  waiting for transfers between devices  47.4 us (40%)
  starting transfers between devices  43.2 us (37%)
  local copies, waits for them, and re-layouts  13.5 us (11%)
  Pallas kernels  10.7 us (9%)
    ppermute x6, waiting for transfers between devices, shards(): minus = lambda v: lax.ppermute(v, 'learn', down)  15.8 us
    ppermute x2, starting transfers between devices, shards(): far = lambda v: lax.ppermute(v, 'learn', across)  15.7 us
    ppermute x6, waiting for transfers between devices, shards(): plus = lambda v: lax.ppermute(v, 'learn', up)  13.6 us
    unnamed x39, local copies, waits for them, and re-layouts  11.6 us
    pallas_call x10, Pallas kernels, call(): pl.pallas_call(body, grid=grid, in_specs=specs + [ANYWHERE] * (n_held + l...  9.79 us
    ppermute x6, starting transfers between devices, shards(): plus = lambda v: lax.ppermute(v, 'learn', up)  8.95 us
    all_to_all x1, starting transfers between devices, shards(): got = lax.all_to_all(parts.astype(BF16), 'tp', 0, 0, tiled=True)  7.62 us
    ppermute x6, starting transfers between devices, shards(): minus = lambda v: lax.ppermute(v, 'learn', down)  5.86 us
  transfers between devices with their start and end apart: 29, of which 17 were waited for; matrix products, arithmetic and copies ran while one was open for 3% of the time, Pallas kernels for 4%

profile of v2, /device:TPU:6, one launch (start us, length us, event | category | flops | bytes accessed | tf_op | source)
XLA Modules:
  0.0 116.0 jit_solution(15443488802012382237)
XLA Ops:
  3.6 1.7 %collective-permute-done.refs_1_ = bf16[512,512]{1,0:T(8,128)(2,1)S(1)} collective-permute-done((bf16[512,512]{1,0:T(8,128)(2,1)S(1)}, bf16[512,512]{1,0:T(8,128)(2,1)S(1)}, u32[]{:S(2)}, u32[]{:S(2)}) %collective-permute-start) | collective-permute-done | bytes 524320 | tf_op jit(solution)/shard_map/ppermute | solution.py:208
  5.3 1.5 %copy-done.2 = bf16[1848,512]{1,0:T(8,128)(2,1)S(1)} copy-done((bf16[1848,512]{1,0:T(8,128)(2,1)S(1)}, bf16[1848,512]{1,0:T(8,128)(2,1)}, u32[]{:S(2)}) %copy-start.2) | copy-done | bytes 1892376
  6.9 1.5 %shard_map.103 = (f32[64,1920]{1,0:T(8,128)S(1)}, f32[64,1920]{1,0:T(8,128)S(1)}, f32[32,1920]{1,0:T(8,128)S(1)}, f32[32,1920]{1,0:T(8,128)S(1)}, f32[64,1920]{1,0:T(8,128)S(1)}) custom-call(bf16[1024,512]{1,0:T(8,128)(2,1)S(1)} %get-tuple-element.27.refs_0_.refs_16_, bf16[512,512]{1,0:T(8,128)(2,1)S(1)} %collective-permute-done.refs_1_, ...), custom_call_target="tpu_custom_call" | custom-call | tf_op jit(solution)/shard_map/pallas_call | solution.py:39
  9.3 2.4 %collective-permute-start.2 = (f32[64,1920]{1,0:T(8,128)S(1)}, f32[64,1920]{1,0:T(8,128)S(1)}, u32[]{:S(2)}, u32[]{:S(2)}) collective-permute-start(f32[64,1920]{1,0:T(8,128)S(1)} %get-tuple-element.29.refs_4_), channel_id=1, source_target_pairs={{0,32},{32,64},{64,96},{96,0},{128,160},{160,192},{192,224},{224,1... | collective-permute-start | bytes 1474568 | tf_op jit(solution)/shard_map/ppermute | solution.py:204
  11.7 1.5 %shard_map.104 = (f32[64,1920]{1,0:T(8,128)S(1)}, f32[64,1920]{1,0:T(8,128)S(1)}, f32[32,1920]{1,0:T(8,128)S(1)}, f32[32,1920]{1,0:T(8,128)S(1)}, f32[64,1920]{1,0:T(8,128)S(1)}) custom-call(bf16[1024,512]{1,0:T(8,128)(2,1)S(1)} %get-tuple-element.27.refs_0_.refs_16_, bf16[512,512]{1,0:T(8,128)(2,1)S(1)} %collective-permute-done.refs_1_, ...), custom_call_target="tpu_custom_call" | custom-call | tf_op jit(solution)/shard_map/pallas_call | solution.py:39
  13.2 9.7 %collective-permute-done.3.refs_3_.refs_2_ = f32[64,1920]{1,0:T(8,128)S(1)} collective-permute-done((f32[64,1920]{1,0:T(8,128)S(1)}, f32[64,1920]{1,0:T(8,128)S(1)}, u32[]{:S(2)}, u32[]{:S(2)}) %collective-permute-start.3) | collective-permute-done | bytes 491552 | tf_op jit(solution)/shard_map/ppermute | solution.py:205
  23.0 3.0 %collective-permute-start.4 = (f32[32,1920]{1,0:T(8,128)S(1)}, f32[32,1920]{1,0:T(8,128)S(1)}, u32[]{:S(2)}, u32[]{:S(2)}) collective-permute-start(f32[32,1920]{1,0:T(8,128)S(1)} %get-tuple-element.36), channel_id=1, source_target_pairs={{0,32},{32,64},{64,96},{96,0},{128,160},{160,192},{192,224},{224,1... | collective-permute-start | bytes 737288 | tf_op jit(solution)/shard_map/ppermute | solution.py:204
  26.1 4.4 %collective-permute-done.4.refs_3_ = f32[32,1920]{1,0:T(8,128)S(1)} collective-permute-done((f32[32,1920]{1,0:T(8,128)S(1)}, f32[32,1920]{1,0:T(8,128)S(1)}, u32[]{:S(2)}, u32[]{:S(2)}) %collective-permute-start.4) | collective-permute-done | bytes 245792 | tf_op jit(solution)/shard_map/ppermute | solution.py:204
  30.5 3.4 %collective-permute-done.5.refs_4_ = f32[32,1920]{1,0:T(8,128)S(1)} collective-permute-done((f32[32,1920]{1,0:T(8,128)S(1)}, f32[32,1920]{1,0:T(8,128)S(1)}, u32[]{:S(2)}, u32[]{:S(2)}) %collective-permute-start.5) | collective-permute-done | bytes 245792 | tf_op jit(solution)/shard_map/ppermute | solution.py:205
  35.0 1.7 %collective-permute-start.7 = (f32[64,1920]{1,0:T(8,128)S(1)}, f32[64,1920]{1,0:T(8,128)S(1)}, u32[]{:S(2)}, u32[]{:S(2)}) collective-permute-start(f32[64,1920]{1,0:T(8,128)S(1)} %get-tuple-element.40), channel_id=1, source_target_pairs={{32,0},{64,32},{96,64},{0,96},{160,128},{192,160},{224,192},{128,2... | collective-permute-start | bytes 1474568 | tf_op jit(solution)/shard_map/ppermute | solution.py:205
  36.8 7.2 %collective-permute-start.10 = (f32[64,1920]{1,0:T(8,128)}, f32[64,1920]{1,0:T(8,128)S(1)}, u32[]{:S(2)}, u32[]{:S(2)}) collective-permute-start(f32[64,1920]{1,0:T(8,128)} %get-tuple-element.45), channel_id=1, source_target_pairs={{0,128},{32,160},{64,192},{96,224},{128,0},{160,32},{192,64},{224,... | collective-permute-start | bytes 1474568 | tf_op jit(solution)/shard_map/ppermute | solution.py:206
  44.0 1.7 %collective-permute-done.6.refs_2_.refs_1_ = f32[64,1920]{1,0:T(8,128)S(1)} collective-permute-done((f32[64,1920]{1,0:T(8,128)S(1)}, f32[64,1920]{1,0:T(8,128)S(1)}, u32[]{:S(2)}, u32[]{:S(2)}) %collective-permute-start.6) | collective-permute-done | bytes 491552 | tf_op jit(solution)/shard_map/ppermute | solution.py:204
  45.7 1.5 %collective-permute-done.7.refs_3_.refs_2_ = f32[64,1920]{1,0:T(8,128)S(1)} collective-permute-done((f32[64,1920]{1,0:T(8,128)S(1)}, f32[64,1920]{1,0:T(8,128)S(1)}, u32[]{:S(2)}, u32[]{:S(2)}) %collective-permute-start.7) | collective-permute-done | bytes 491552 | tf_op jit(solution)/shard_map/ppermute | solution.py:205
  48.3 1.7 %collective-permute-start.9 = (f32[32,1920]{1,0:T(8,128)}, f32[32,1920]{1,0:T(8,128)S(1)}, u32[]{:S(2)}, u32[]{:S(2)}) collective-permute-start(f32[32,1920]{1,0:T(8,128)} %get-tuple-element.44), channel_id=1, source_target_pairs={{32,0},{64,32},{96,64},{0,96},{160,128},{192,160},{224,192},{128,2... | collective-permute-start | bytes 737288 | tf_op jit(solution)/shard_map/ppermute | solution.py:205
  50.2 4.3 %collective-permute-done.8.refs_3_ = f32[32,1920]{1,0:T(8,128)S(1)} collective-permute-done((f32[32,1920]{1,0:T(8,128)}, f32[32,1920]{1,0:T(8,128)S(1)}, u32[]{:S(2)}, u32[]{:S(2)}) %collective-permute-start.8) | collective-permute-done | bytes 245792 | tf_op jit(solution)/shard_map/ppermute | solution.py:204
  61.3 2.4 %collective-permute-start.12 = (bf16[64,1920]{1,0:T(8,128)(2,1)S(1)}, bf16[64,1920]{1,0:T(8,128)(2,1)S(1)}, u32[]{:S(2)}, u32[]{:S(2)}) collective-permute-start(bf16[64,1920]{1,0:T(8,128)(2,1)S(1)} %shard_map.109.refs_5_.refs_0_), channel_id=1, source_target_pairs={{0,32},{32,64},{64,96},{96,0},{128,160},{160,192},{192,224},{224,1... | collective-permute-start | bytes 737288 | tf_op jit(solution)/shard_map/ppermute | solution.py:204
  63.7 8.5 %collective-permute-start.14 = (bf16[64,1920]{1,0:T(8,128)(2,1)S(1)}, bf16[64,1920]{1,0:T(8,128)(2,1)S(1)}, u32[]{:S(2)}, u32[]{:S(2)}) collective-permute-start(bf16[64,1920]{1,0:T(8,128)(2,1)S(1)} %shard_map.109.refs_5_.refs_0_), channel_id=1, source_target_pairs={{0,128},{32,160},{64,192},{96,224},{128,0},{160,32},{192,64},{224,... | collective-permute-start | bytes 737288 | tf_op jit(solution)/shard_map/ppermute | solution.py:206
  75.0 4.6 %collective-permute-done.14.refs_0_ = bf16[64,1920]{1,0:T(8,128)(2,1)S(1)} collective-permute-done((bf16[64,1920]{1,0:T(8,128)(2,1)S(1)}, bf16[64,1920]{1,0:T(8,128)(2,1)S(1)}, u32[]{:S(2)}, u32[]{:S(2)}) %collective-permute-start.14) | collective-permute-done | bytes 245792 | tf_op jit(solution)/shard_map/ppermute | solution.py:206
  79.6 1.7 %collective-permute-start.18 = (bf16[64,1920]{1,0:T(8,128)(2,1)S(1)}, bf16[64,1920]{1,0:T(8,128)(2,1)S(1)}, u32[]{:S(2)}, u32[]{:S(2)}) collective-permute-start(bf16[64,1920]{1,0:T(8,128)(2,1)S(1)} %shard_map.111.refs_4_), channel_id=1, source_target_pairs={{0,64},{32,96},{64,0},{96,32},{128,192},{160,224},{192,128},{224,1... | collective-permute-start | bytes 737288 | tf_op jit(solution)/shard_map/ppermute | solution.py:207
  83.8 3.8 %collective-permute-done.18.refs_7_ = bf16[64,1920]{1,0:T(8,128)(2,1)S(1)} collective-permute-done((bf16[64,1920]{1,0:T(8,128)(2,1)S(1)}, bf16[64,1920]{1,0:T(8,128)(2,1)S(1)}, u32[]{:S(2)}, u32[]{:S(2)}) %collective-permute-start.18) | collective-permute-done | bytes 245792 | tf_op jit(solution)/shard_map/ppermute | solution.py:207
  87.6 3.1 %collective-permute-done.17.refs_6_ = bf16[64,1920]{1,0:T(8,128)(2,1)S(1)} collective-permute-done((bf16[64,1920]{1,0:T(8,128)(2,1)S(1)}, bf16[64,1920]{1,0:T(8,128)(2,1)S(1)}, u32[]{:S(2)}, u32[]{:S(2)}) %collective-permute-start.17) | collective-permute-done | bytes 245792 | tf_op jit(solution)/shard_map/ppermute | solution.py:204
  92.6 4.1 %shard_map.112 = (bf16[1848,512]{1,0:T(8,128)(2,1)S(1)}, f32[128,512]{1,0:T(8,128)S(1)}) custom-call(bf16[64,1920]{1,0:T(8,128)(2,1)S(1)} %shard_map.109.refs_5_.refs_0_, bf16[64,1920]{1,0:T(8,128)(2,1)S(1)} %collective-permute-done.11.refs_2_.refs_1_, bf16[64,1920]{1,0:T(8,128)(2,1)S(1)} %collective-permute-done.12.refs_1_.refs_2_, ...), custom_call_target="tpu_custom_call" | custom-call | tf_op jit(solution)/shard_map/pallas_call | solution.py:39
  99.2 7.6 %all-to-all-start = ((bf16[16,32,128]{2,1,0:T(8,128)(2,1)}), bf16[16,32,128]{2,1,0:T(8,128)(2,1)S(1)}, u32[]{:S(2)}, u32[]{:S(2)}) async-start(bf16[16,32,128]{2,1,0:T(8,128)(2,1)} %convert_element_type.16), calls=%async_computation | async-start | bytes 262144 | tf_op jit(solution)/shard_map/all_to_all | solution.py:248
  109.6 5.7 %all-to-all-done = bf16[16,32,128]{2,1,0:T(8,128)(2,1)S(1)} async-done(((bf16[16,32,128]{2,1,0:T(8,128)(2,1)}), bf16[16,32,128]{2,1,0:T(8,128)(2,1)S(1)}, u32[]{:S(2)}, u32[]{:S(2)}) %all-to-all-start) | async-done | bytes 131104 | tf_op jit(solution)/shard_map/all_to_all | solution.py:248
  (95 shorter events, 26.2 us)
Async XLA Ops:
  0.6 4.7 %collective-permute-start.1 = (bf16[1848,512]{1,0:T(8,128)(2,1)}, bf16[1848,512]{1,0:T(8,128)(2,1)S(1)}, u32[]{:S(2)}, u32[]{:S(2)}) collective-permute-start(bf16[1848,512]{1,0:T(8,128)(2,1)} %refs_2_.3), channel_id=1, source_target_pairs={{0,1},{1,0},{2,3},{3,2},{4,5},{5,4},{6,7},{7,6},{8,9},{9,8},{10,11... | collective-permute-start | bytes 5677064 | tf_op jit(solution)/shard_map/ppermute | solution.py:208
  8.4 14.6 %collective-permute-start.3 = (f32[64,1920]{1,0:T(8,128)S(1)}, f32[64,1920]{1,0:T(8,128)S(1)}, u32[]{:S(2)}, u32[]{:S(2)}) collective-permute-start(f32[64,1920]{1,0:T(8,128)S(1)} %get-tuple-element.32), channel_id=1, source_target_pairs={{32,0},{64,32},{96,64},{0,96},{160,128},{192,160},{224,192},{128,2... | collective-permute-start | bytes 1474568 | tf_op jit(solution)/shard_map/ppermute | solution.py:205
  9.3 13.7 %collective-permute-start.2 = (f32[64,1920]{1,0:T(8,128)S(1)}, f32[64,1920]{1,0:T(8,128)S(1)}, u32[]{:S(2)}, u32[]{:S(2)}) collective-permute-start(f32[64,1920]{1,0:T(8,128)S(1)} %get-tuple-element.29.refs_4_), channel_id=1, source_target_pairs={{0,32},{32,64},{64,96},{96,0},{128,160},{160,192},{192,224},{224,1... | collective-permute-start | bytes 1474568 | tf_op jit(solution)/shard_map/ppermute | solution.py:204
  23.0 7.4 %collective-permute-start.4 = (f32[32,1920]{1,0:T(8,128)S(1)}, f32[32,1920]{1,0:T(8,128)S(1)}, u32[]{:S(2)}, u32[]{:S(2)}) collective-permute-start(f32[32,1920]{1,0:T(8,128)S(1)} %get-tuple-element.36), channel_id=1, source_target_pairs={{0,32},{32,64},{64,96},{96,0},{128,160},{160,192},{192,224},{224,1... | collective-permute-start | bytes 737288 | tf_op jit(solution)/shard_map/ppermute | solution.py:204
  26.1 7.8 %collective-permute-start.5 = (f32[32,1920]{1,0:T(8,128)S(1)}, f32[32,1920]{1,0:T(8,128)S(1)}, u32[]{:S(2)}, u32[]{:S(2)}) collective-permute-start(f32[32,1920]{1,0:T(8,128)S(1)} %get-tuple-element.37), channel_id=1, source_target_pairs={{32,0},{64,32},{96,64},{0,96},{160,128},{192,160},{224,192},{128,2... | collective-permute-start | bytes 737288 | tf_op jit(solution)/shard_map/ppermute | solution.py:205
  34.8 11.0 %collective-permute-start.6 = (f32[64,1920]{1,0:T(8,128)S(1)}, f32[64,1920]{1,0:T(8,128)S(1)}, u32[]{:S(2)}, u32[]{:S(2)}) collective-permute-start(f32[64,1920]{1,0:T(8,128)S(1)} %get-tuple-element.39), channel_id=1, source_target_pairs={{0,32},{32,64},{64,96},{96,0},{128,160},{160,192},{192,224},{224,1... | collective-permute-start | bytes 1474568 | tf_op jit(solution)/shard_map/ppermute | solution.py:204
  35.0 12.2 %collective-permute-start.7 = (f32[64,1920]{1,0:T(8,128)S(1)}, f32[64,1920]{1,0:T(8,128)S(1)}, u32[]{:S(2)}, u32[]{:S(2)}) collective-permute-start(f32[64,1920]{1,0:T(8,128)S(1)} %get-tuple-element.40), channel_id=1, source_target_pairs={{32,0},{64,32},{96,64},{0,96},{160,128},{192,160},{224,192},{128,2... | collective-permute-start | bytes 1474568 | tf_op jit(solution)/shard_map/ppermute | solution.py:205
  36.8 22.9 %collective-permute-start.10 = (f32[64,1920]{1,0:T(8,128)}, f32[64,1920]{1,0:T(8,128)S(1)}, u32[]{:S(2)}, u32[]{:S(2)}) collective-permute-start(f32[64,1920]{1,0:T(8,128)} %get-tuple-element.45), channel_id=1, source_target_pairs={{0,128},{32,160},{64,192},{96,224},{128,0},{160,32},{192,64},{224,... | collective-permute-start | bytes 1474568 | tf_op jit(solution)/shard_map/ppermute | solution.py:206
  48.1 6.4 %collective-permute-start.8 = (f32[32,1920]{1,0:T(8,128)}, f32[32,1920]{1,0:T(8,128)S(1)}, u32[]{:S(2)}, u32[]{:S(2)}) collective-permute-start(f32[32,1920]{1,0:T(8,128)} %get-tuple-element.43), channel_id=1, source_target_pairs={{0,32},{32,64},{64,96},{96,0},{128,160},{160,192},{192,224},{224,1... | collective-permute-start | bytes 737288 | tf_op jit(solution)/shard_map/ppermute | solution.py:204
  48.3 7.6 %collective-permute-start.9 = (f32[32,1920]{1,0:T(8,128)}, f32[32,1920]{1,0:T(8,128)S(1)}, u32[]{:S(2)}, u32[]{:S(2)}) collective-permute-start(f32[32,1920]{1,0:T(8,128)} %get-tuple-element.44), channel_id=1, source_target_pairs={{32,0},{64,32},{96,64},{0,96},{160,128},{192,160},{224,192},{128,2... | collective-permute-start | bytes 737288 | tf_op jit(solution)/shard_map/ppermute | solution.py:205
  50.1 22.1 %collective-permute-start.15 = (bf16[64,1848]{1,0:T(8,128)(2,1)}, bf16[64,1848]{1,0:T(8,128)(2,1)S(1)}, u32[]{:S(2)}, u32[]{:S(2)}) collective-permute-start(bf16[64,1848]{1,0:T(8,128)(2,1)} %refs_18_.1), channel_id=1, source_target_pairs={{0,1},{1,0},{2,3},{3,2},{4,5},{5,4},{6,7},{7,6},{8,9},{9,8},{10,11... | collective-permute-start | bytes 709640 | tf_op jit(solution)/shard_map/ppermute | solution.py:208
  60.2 14.0 %collective-permute-start.13 = (bf16[64,1920]{1,0:T(8,128)(2,1)S(1)}, bf16[64,1920]{1,0:T(8,128)(2,1)S(1)}, u32[]{:S(2)}, u32[]{:S(2)}) collective-permute-start(bf16[64,1920]{1,0:T(8,128)(2,1)S(1)} %shard_map.109.refs_5_.refs_0_), channel_id=1, source_target_pairs={{0,64},{32,96},{64,0},{96,32},{128,192},{160,224},{192,128},{224,1... | collective-permute-start | bytes 737288 | tf_op jit(solution)/shard_map/ppermute | solution.py:207
  61.3 13.5 %collective-permute-start.12 = (bf16[64,1920]{1,0:T(8,128)(2,1)S(1)}, bf16[64,1920]{1,0:T(8,128)(2,1)S(1)}, u32[]{:S(2)}, u32[]{:S(2)}) collective-permute-start(bf16[64,1920]{1,0:T(8,128)(2,1)S(1)} %shard_map.109.refs_5_.refs_0_), channel_id=1, source_target_pairs={{0,32},{32,64},{64,96},{96,0},{128,160},{160,192},{192,224},{224,1... | collective-permute-start | bytes 737288 | tf_op jit(solution)/shard_map/ppermute | solution.py:204
  63.7 15.8 %collective-permute-start.14 = (bf16[64,1920]{1,0:T(8,128)(2,1)S(1)}, bf16[64,1920]{1,0:T(8,128)(2,1)S(1)}, u32[]{:S(2)}, u32[]{:S(2)}) collective-permute-start(bf16[64,1920]{1,0:T(8,128)(2,1)S(1)} %shard_map.109.refs_5_.refs_0_), channel_id=1, source_target_pairs={{0,128},{32,160},{64,192},{96,224},{128,0},{160,32},{192,64},{224,... | collective-permute-start | bytes 737288 | tf_op jit(solution)/shard_map/ppermute | solution.py:206
  72.2 7.4 %collective-permute-start.11 = (bf16[64,1920]{1,0:T(8,128)(2,1)S(1)}, bf16[64,1920]{1,0:T(8,128)(2,1)S(1)}, u32[]{:S(2)}, u32[]{:S(2)}) collective-permute-start(bf16[64,1920]{1,0:T(8,128)(2,1)S(1)} %shard_map.109.refs_5_.refs_0_), channel_id=1, source_target_pairs={{32,0},{64,32},{96,64},{0,96},{160,128},{192,160},{224,192},{128,2... | collective-permute-start | bytes 737288 | tf_op jit(solution)/shard_map/ppermute | solution.py:205
  72.9 8.9 %collective-permute-start.19 = (bf16[64,1920]{1,0:T(8,128)(2,1)S(1)}, bf16[64,1920]{1,0:T(8,128)(2,1)S(1)}, u32[]{:S(2)}, u32[]{:S(2)}) collective-permute-start(bf16[64,1920]{1,0:T(8,128)(2,1)S(1)} %shard_map.109.refs_5_.refs_0_), channel_id=1, source_target_pairs={{0,1},{1,0},{2,3},{3,2},{4,5},{5,4},{6,7},{7,6},{8,9},{9,8},{10,11... | collective-permute-start | bytes 737288 | tf_op jit(solution)/shard_map/ppermute | solution.py:208
  74.3 9.0 %collective-permute-start.22 = (bf16[64,1920]{1,0:T(8,128)(2,1)S(1)}, bf16[64,1920]{1,0:T(8,128)(2,1)S(1)}, u32[]{:S(2)}, u32[]{:S(2)}) collective-permute-start(bf16[64,1920]{1,0:T(8,128)(2,1)S(1)} %collective-permute-done.13.refs_3_), channel_id=1, source_target_pairs={{0,1},{1,0},{2,3},{3,2},{4,5},{5,4},{6,7},{7,6},{8,9},{9,8},{10,11... | collective-permute-start | bytes 737288 | tf_op jit(solution)/shard_map/ppermute | solution.py:208
  74.9 8.4 %collective-permute-start.21 = (bf16[64,1920]{1,0:T(8,128)(2,1)S(1)}, bf16[64,1920]{1,0:T(8,128)(2,1)S(1)}, u32[]{:S(2)}, u32[]{:S(2)}) collective-permute-start(bf16[64,1920]{1,0:T(8,128)(2,1)S(1)} %collective-permute-done.12.refs_1_.refs_2_), channel_id=1, source_target_pairs={{0,1},{1,0},{2,3},{3,2},{4,5},{5,4},{6,7},{7,6},{8,9},{9,8},{10,11... | collective-permute-start | bytes 737288 | tf_op jit(solution)/shard_map/ppermute | solution.py:208
  79.6 8.0 %collective-permute-start.18 = (bf16[64,1920]{1,0:T(8,128)(2,1)S(1)}, bf16[64,1920]{1,0:T(8,128)(2,1)S(1)}, u32[]{:S(2)}, u32[]{:S(2)}) collective-permute-start(bf16[64,1920]{1,0:T(8,128)(2,1)S(1)} %shard_map.111.refs_4_), channel_id=1, source_target_pairs={{0,64},{32,96},{64,0},{96,32},{128,192},{160,224},{192,128},{224,1... | collective-permute-start | bytes 737288 | tf_op jit(solution)/shard_map/ppermute | solution.py:207
  81.3 9.4 %collective-permute-start.17 = (bf16[64,1920]{1,0:T(8,128)(2,1)S(1)}, bf16[64,1920]{1,0:T(8,128)(2,1)S(1)}, u32[]{:S(2)}, u32[]{:S(2)}) collective-permute-start(bf16[64,1920]{1,0:T(8,128)(2,1)S(1)} %shard_map.111.refs_4_), channel_id=1, source_target_pairs={{0,32},{32,64},{64,96},{96,0},{128,160},{160,192},{192,224},{224,1... | collective-permute-start | bytes 737288 | tf_op jit(solution)/shard_map/ppermute | solution.py:204
  81.8 9.2 %collective-permute-start.16 = (bf16[64,1920]{1,0:T(8,128)(2,1)S(1)}, bf16[64,1920]{1,0:T(8,128)(2,1)S(1)}, u32[]{:S(2)}, u32[]{:S(2)}) collective-permute-start(bf16[64,1920]{1,0:T(8,128)(2,1)S(1)} %shard_map.111.refs_4_), channel_id=1, source_target_pairs={{32,0},{64,32},{96,64},{0,96},{160,128},{192,160},{224,192},{128,2... | collective-permute-start | bytes 737288 | tf_op jit(solution)/shard_map/ppermute | solution.py:205
  83.3 7.9 %collective-permute-start.23 = (bf16[64,1920]{1,0:T(8,128)(2,1)S(1)}, bf16[64,1920]{1,0:T(8,128)(2,1)S(1)}, u32[]{:S(2)}, u32[]{:S(2)}) collective-permute-start(bf16[64,1920]{1,0:T(8,128)(2,1)S(1)} %shard_map.111.refs_4_), channel_id=1, source_target_pairs={{0,1},{1,0},{2,3},{3,2},{4,5},{5,4},{6,7},{7,6},{8,9},{9,8},{10,11... | collective-permute-start | bytes 737288 | tf_op jit(solution)/shard_map/ppermute | solution.py:208
  83.3 7.9 %collective-permute-start.20 = (bf16[64,1920]{1,0:T(8,128)(2,1)S(1)}, bf16[64,1920]{1,0:T(8,128)(2,1)S(1)}, u32[]{:S(2)}, u32[]{:S(2)}) collective-permute-start(bf16[64,1920]{1,0:T(8,128)(2,1)S(1)} %collective-permute-done.11.refs_2_.refs_1_), channel_id=1, source_target_pairs={{0,1},{1,0},{2,3},{3,2},{4,5},{5,4},{6,7},{7,6},{8,9},{9,8},{10,11... | collective-permute-start | bytes 737288 | tf_op jit(solution)/shard_map/ppermute | solution.py:208
  99.2 16.1 %all-to-all-start = ((bf16[16,32,128]{2,1,0:T(8,128)(2,1)}), bf16[16,32,128]{2,1,0:T(8,128)(2,1)S(1)}, u32[]{:S(2)}, u32[]{:S(2)}) async-start(bf16[16,32,128]{2,1,0:T(8,128)(2,1)} %convert_element_type.16), calls=%async_computation | async-start | bytes 262144 | tf_op jit(solution)/shard_map/all_to_all | solution.py:248
  (23 other events, 174.0 us)

commit v3 on v2

--- a/solution.py
+++ b/solution.py
@@ -12,7 +12,7 @@
 ADAM_EPS = 1e-06
 STEP_RATE = 0.01
 RING = 4
-ROWS = 384
+ROWS = 1024
 VMEM = 16 * 2**20
 F32 = jnp.float32
 BF16 = jnp.bfloat16

time: 118 us -> 117 us (level)
  transfers between devices with their start and end apart: 29 -> 29, of which waited for: 17 -> 17; matrix products, arithmetic and copies ran while one was open for 3% -> 3% of each run, Pallas kernels for 4% -> 3%
where the time goes in v3:
time: 117 us; the launch traced here: 115 us
  waiting for transfers between devices  47.6 us (41%)
  starting transfers between devices  43 us (37%)
  local copies, waits for them, and re-layouts  13.5 us (12%)
  Pallas kernels  9.72 us (8%)
    ppermute x6, waiting for transfers between devices, shards(): minus = lambda v: lax.ppermute(v, 'learn', down)  16 us
    ppermute x2, starting transfers between devices, shards(): far = lambda v: lax.ppermute(v, 'learn', across)  15.7 us
    ppermute x6, waiting for transfers between devices, shards(): plus = lambda v: lax.ppermute(v, 'learn', up)  13.5 us
    unnamed x39, local copies, waits for them, and re-layouts  11.6 us
    ppermute x6, starting transfers between devices, shards(): plus = lambda v: lax.ppermute(v, 'learn', up)  8.82 us
    pallas_call x10, Pallas kernels, call(): pl.pallas_call(body, grid=grid, in_specs=specs + [ANYWHERE] * (n_held + l...  8.75 us
    all_to_all x1, starting transfers between devices, shards(): got = lax.all_to_all(parts.astype(BF16), 'tp', 0, 0, tiled=True)  7.56 us
    ppermute x6, starting transfers between devices, shards(): minus = lambda v: lax.ppermute(v, 'learn', down)  5.99 us
  transfers between devices with their start and end apart: 29, of which 17 were waited for; matrix products, arithmetic and copies ran while one was open for 3% of the time, Pallas kernels for 3%

profile of v3, /device:TPU:6, one launch (start us, length us, event | category | flops | bytes accessed | tf_op | source)
XLA Modules:
  0.0 115.0 jit_solution(6694923321176775711)
XLA Ops:
  3.6 1.7 %collective-permute-done.refs_1_ = bf16[512,512]{1,0:T(8,128)(2,1)S(1)} collective-permute-done((bf16[512,512]{1,0:T(8,128)(2,1)S(1)}, bf16[512,512]{1,0:T(8,128)(2,1)S(1)}, u32[]{:S(2)}, u32[]{:S(2)}) %collective-permute-start) | collective-permute-done | bytes 524320 | tf_op jit(solution)/shard_map/ppermute | solution.py:208
  5.3 1.5 %copy-done.2 = bf16[1848,512]{1,0:T(8,128)(2,1)S(1)} copy-done((bf16[1848,512]{1,0:T(8,128)(2,1)S(1)}, bf16[1848,512]{1,0:T(8,128)(2,1)}, u32[]{:S(2)}) %copy-start.2) | copy-done | bytes 1892376
  9.0 2.4 %collective-permute-start.2 = (f32[64,1920]{1,0:T(8,128)S(1)}, f32[64,1920]{1,0:T(8,128)S(1)}, u32[]{:S(2)}, u32[]{:S(2)}) collective-permute-start(f32[64,1920]{1,0:T(8,128)S(1)} %get-tuple-element.29.refs_4_), channel_id=1, source_target_pairs={{0,32},{32,64},{64,96},{96,0},{128,160},{160,192},{192,224},{224,1... | collective-permute-start | bytes 1474568 | tf_op jit(solution)/shard_map/ppermute | solution.py:204
  11.5 1.3 %shard_map.104 = (f32[64,1920]{1,0:T(8,128)S(1)}, f32[64,1920]{1,0:T(8,128)S(1)}, f32[32,1920]{1,0:T(8,128)S(1)}, f32[32,1920]{1,0:T(8,128)S(1)}, f32[64,1920]{1,0:T(8,128)S(1)}) custom-call(bf16[1024,512]{1,0:T(8,128)(2,1)S(1)} %get-tuple-element.27.refs_0_.refs_16_, bf16[512,512]{1,0:T(8,128)(2,1)S(1)} %collective-permute-done.refs_1_, ...), custom_call_target="tpu_custom_call" | custom-call | tf_op jit(solution)/shard_map/pallas_call | solution.py:39
  12.7 10.0 %collective-permute-done.3.refs_3_.refs_2_ = f32[64,1920]{1,0:T(8,128)S(1)} collective-permute-done((f32[64,1920]{1,0:T(8,128)S(1)}, f32[64,1920]{1,0:T(8,128)S(1)}, u32[]{:S(2)}, u32[]{:S(2)}) %collective-permute-start.3) | collective-permute-done | bytes 491552 | tf_op jit(solution)/shard_map/ppermute | solution.py:205
  22.8 3.0 %collective-permute-start.4 = (f32[32,1920]{1,0:T(8,128)S(1)}, f32[32,1920]{1,0:T(8,128)S(1)}, u32[]{:S(2)}, u32[]{:S(2)}) collective-permute-start(f32[32,1920]{1,0:T(8,128)S(1)} %get-tuple-element.36), channel_id=1, source_target_pairs={{0,32},{32,64},{64,96},{96,0},{128,160},{160,192},{192,224},{224,1... | collective-permute-start | bytes 737288 | tf_op jit(solution)/shard_map/ppermute | solution.py:204
  25.8 4.4 %collective-permute-done.4.refs_3_ = f32[32,1920]{1,0:T(8,128)S(1)} collective-permute-done((f32[32,1920]{1,0:T(8,128)S(1)}, f32[32,1920]{1,0:T(8,128)S(1)}, u32[]{:S(2)}, u32[]{:S(2)}) %collective-permute-start.4) | collective-permute-done | bytes 245792 | tf_op jit(solution)/shard_map/ppermute | solution.py:204
  30.2 3.4 %collective-permute-done.5.refs_4_ = f32[32,1920]{1,0:T(8,128)S(1)} collective-permute-done((f32[32,1920]{1,0:T(8,128)S(1)}, f32[32,1920]{1,0:T(8,128)S(1)}, u32[]{:S(2)}, u32[]{:S(2)}) %collective-permute-start.5) | collective-permute-done | bytes 245792 | tf_op jit(solution)/shard_map/ppermute | solution.py:205
  34.8 1.7 %collective-permute-start.7 = (f32[64,1920]{1,0:T(8,128)S(1)}, f32[64,1920]{1,0:T(8,128)S(1)}, u32[]{:S(2)}, u32[]{:S(2)}) collective-permute-start(f32[64,1920]{1,0:T(8,128)S(1)} %get-tuple-element.40), channel_id=1, source_target_pairs={{32,0},{64,32},{96,64},{0,96},{160,128},{192,160},{224,192},{128,2... | collective-permute-start | bytes 1474568 | tf_op jit(solution)/shard_map/ppermute | solution.py:205
  36.5 7.2 %collective-permute-start.10 = (f32[64,1920]{1,0:T(8,128)}, f32[64,1920]{1,0:T(8,128)S(1)}, u32[]{:S(2)}, u32[]{:S(2)}) collective-permute-start(f32[64,1920]{1,0:T(8,128)} %get-tuple-element.45), channel_id=1, source_target_pairs={{0,128},{32,160},{64,192},{96,224},{128,0},{160,32},{192,64},{224,... | collective-permute-start | bytes 1474568 | tf_op jit(solution)/shard_map/ppermute | solution.py:206
  43.7 1.7 %collective-permute-done.6.refs_2_.refs_1_ = f32[64,1920]{1,0:T(8,128)S(1)} collective-permute-done((f32[64,1920]{1,0:T(8,128)S(1)}, f32[64,1920]{1,0:T(8,128)S(1)}, u32[]{:S(2)}, u32[]{:S(2)}) %collective-permute-start.6) | collective-permute-done | bytes 491552 | tf_op jit(solution)/shard_map/ppermute | solution.py:204
  45.4 1.5 %collective-permute-done.7.refs_3_.refs_2_ = f32[64,1920]{1,0:T(8,128)S(1)} collective-permute-done((f32[64,1920]{1,0:T(8,128)S(1)}, f32[64,1920]{1,0:T(8,128)S(1)}, u32[]{:S(2)}, u32[]{:S(2)}) %collective-permute-start.7) | collective-permute-done | bytes 491552 | tf_op jit(solution)/shard_map/ppermute | solution.py:205
  48.1 1.7 %collective-permute-start.9 = (f32[32,1920]{1,0:T(8,128)}, f32[32,1920]{1,0:T(8,128)S(1)}, u32[]{:S(2)}, u32[]{:S(2)}) collective-permute-start(f32[32,1920]{1,0:T(8,128)} %get-tuple-element.44), channel_id=1, source_target_pairs={{32,0},{64,32},{96,64},{0,96},{160,128},{192,160},{224,192},{128,2... | collective-permute-start | bytes 737288 | tf_op jit(solution)/shard_map/ppermute | solution.py:205
  49.9 4.3 %collective-permute-done.8.refs_3_ = f32[32,1920]{1,0:T(8,128)S(1)} collective-permute-done((f32[32,1920]{1,0:T(8,128)}, f32[32,1920]{1,0:T(8,128)S(1)}, u32[]{:S(2)}, u32[]{:S(2)}) %collective-permute-start.8) | collective-permute-done | bytes 245792 | tf_op jit(solution)/shard_map/ppermute | solution.py:204
  60.9 2.4 %collective-permute-start.12 = (bf16[64,1920]{1,0:T(8,128)(2,1)S(1)}, bf16[64,1920]{1,0:T(8,128)(2,1)S(1)}, u32[]{:S(2)}, u32[]{:S(2)}) collective-permute-start(bf16[64,1920]{1,0:T(8,128)(2,1)S(1)} %shard_map.109.refs_5_.refs_0_), channel_id=1, source_target_pairs={{0,32},{32,64},{64,96},{96,0},{128,160},{160,192},{192,224},{224,1... | collective-permute-start | bytes 737288 | tf_op jit(solution)/shard_map/ppermute | solution.py:204
  63.2 8.5 %collective-permute-start.14 = (bf16[64,1920]{1,0:T(8,128)(2,1)S(1)}, bf16[64,1920]{1,0:T(8,128)(2,1)S(1)}, u32[]{:S(2)}, u32[]{:S(2)}) collective-permute-start(bf16[64,1920]{1,0:T(8,128)(2,1)S(1)} %shard_map.109.refs_5_.refs_0_), channel_id=1, source_target_pairs={{0,128},{32,160},{64,192},{96,224},{128,0},{160,32},{192,64},{224,... | collective-permute-start | bytes 737288 | tf_op jit(solution)/shard_map/ppermute | solution.py:206
  74.5 4.6 %collective-permute-done.14.refs_0_ = bf16[64,1920]{1,0:T(8,128)(2,1)S(1)} collective-permute-done((bf16[64,1920]{1,0:T(8,128)(2,1)S(1)}, bf16[64,1920]{1,0:T(8,128)(2,1)S(1)}, u32[]{:S(2)}, u32[]{:S(2)}) %collective-permute-start.14) | collective-permute-done | bytes 245792 | tf_op jit(solution)/shard_map/ppermute | solution.py:206
  79.2 1.7 %collective-permute-start.18 = (bf16[64,1920]{1,0:T(8,128)(2,1)S(1)}, bf16[64,1920]{1,0:T(8,128)(2,1)S(1)}, u32[]{:S(2)}, u32[]{:S(2)}) collective-permute-start(bf16[64,1920]{1,0:T(8,128)(2,1)S(1)} %shard_map.111.refs_4_), channel_id=1, source_target_pairs={{0,64},{32,96},{64,0},{96,32},{128,192},{160,224},{192,128},{224,1... | collective-permute-start | bytes 737288 | tf_op jit(solution)/shard_map/ppermute | solution.py:207
  81.3 1.6 %collective-permute-start.16 = (bf16[64,1920]{1,0:T(8,128)(2,1)S(1)}, bf16[64,1920]{1,0:T(8,128)(2,1)S(1)}, u32[]{:S(2)}, u32[]{:S(2)}) collective-permute-start(bf16[64,1920]{1,0:T(8,128)(2,1)S(1)} %shard_map.111.refs_4_), channel_id=1, source_target_pairs={{32,0},{64,32},{96,64},{0,96},{160,128},{192,160},{224,192},{128,2... | collective-permute-start | bytes 737288 | tf_op jit(solution)/shard_map/ppermute | solution.py:205
  83.4 3.7 %collective-permute-done.18.refs_7_ = bf16[64,1920]{1,0:T(8,128)(2,1)S(1)} collective-permute-done((bf16[64,1920]{1,0:T(8,128)(2,1)S(1)}, bf16[64,1920]{1,0:T(8,128)(2,1)S(1)}, u32[]{:S(2)}, u32[]{:S(2)}) %collective-permute-start.18) | collective-permute-done | bytes 245792 | tf_op jit(solution)/shard_map/ppermute | solution.py:207
  87.1 3.1 %collective-permute-done.17.refs_6_ = bf16[64,1920]{1,0:T(8,128)(2,1)S(1)} collective-permute-done((bf16[64,1920]{1,0:T(8,128)(2,1)S(1)}, bf16[64,1920]{1,0:T(8,128)(2,1)S(1)}, u32[]{:S(2)}, u32[]{:S(2)}) %collective-permute-start.17) | collective-permute-done | bytes 245792 | tf_op jit(solution)/shard_map/ppermute | solution.py:204
  92.1 3.6 %shard_map.112 = (bf16[1848,512]{1,0:T(8,128)(2,1)S(1)}, f32[128,512]{1,0:T(8,128)S(1)}) custom-call(bf16[64,1920]{1,0:T(8,128)(2,1)S(1)} %shard_map.109.refs_5_.refs_0_, bf16[64,1920]{1,0:T(8,128)(2,1)S(1)} %collective-permute-done.11.refs_2_.refs_1_, bf16[64,1920]{1,0:T(8,128)(2,1)S(1)} %collective-permute-done.12.refs_1_.refs_2_, ...), custom_call_target="tpu_custom_call" | custom-call | tf_op jit(solution)/shard_map/pallas_call | solution.py:39
  98.2 7.6 %all-to-all-start = ((bf16[16,32,128]{2,1,0:T(8,128)(2,1)}), bf16[16,32,128]{2,1,0:T(8,128)(2,1)S(1)}, u32[]{:S(2)}, u32[]{:S(2)}) async-start(bf16[16,32,128]{2,1,0:T(8,128)(2,1)} %convert_element_type.16), calls=%async_computation | async-start | bytes 262144 | tf_op jit(solution)/shard_map/all_to_all | solution.py:248
  108.5 5.7 %all-to-all-done = bf16[16,32,128]{2,1,0:T(8,128)(2,1)S(1)} async-done(((bf16[16,32,128]{2,1,0:T(8,128)(2,1)}), bf16[16,32,128]{2,1,0:T(8,128)(2,1)S(1)}, u32[]{:S(2)}, u32[]{:S(2)}) %all-to-all-start) | async-done | bytes 131104 | tf_op jit(solution)/shard_map/all_to_all | solution.py:248
  (95 shorter events, 25.7 us)
Async XLA Ops:
  0.6 4.7 %collective-permute-start.1 = (bf16[1848,512]{1,0:T(8,128)(2,1)}, bf16[1848,512]{1,0:T(8,128)(2,1)S(1)}, u32[]{:S(2)}, u32[]{:S(2)}) collective-permute-start(bf16[1848,512]{1,0:T(8,128)(2,1)} %refs_2_.3), channel_id=1, source_target_pairs={{0,1},{1,0},{2,3},{3,2},{4,5},{5,4},{6,7},{7,6},{8,9},{9,8},{10,11... | collective-permute-start | bytes 5677064 | tf_op jit(solution)/shard_map/ppermute | solution.py:208
  8.1 14.6 %collective-permute-start.3 = (f32[64,1920]{1,0:T(8,128)S(1)}, f32[64,1920]{1,0:T(8,128)S(1)}, u32[]{:S(2)}, u32[]{:S(2)}) collective-permute-start(f32[64,1920]{1,0:T(8,128)S(1)} %get-tuple-element.32), channel_id=1, source_target_pairs={{32,0},{64,32},{96,64},{0,96},{160,128},{192,160},{224,192},{128,2... | collective-permute-start | bytes 1474568 | tf_op jit(solution)/shard_map/ppermute | solution.py:205
  9.0 13.7 %collective-permute-start.2 = (f32[64,1920]{1,0:T(8,128)S(1)}, f32[64,1920]{1,0:T(8,128)S(1)}, u32[]{:S(2)}, u32[]{:S(2)}) collective-permute-start(f32[64,1920]{1,0:T(8,128)S(1)} %get-tuple-element.29.refs_4_), channel_id=1, source_target_pairs={{0,32},{32,64},{64,96},{96,0},{128,160},{160,192},{192,224},{224,1... | collective-permute-start | bytes 1474568 | tf_op jit(solution)/shard_map/ppermute | solution.py:204
  22.8 7.4 %collective-permute-start.4 = (f32[32,1920]{1,0:T(8,128)S(1)}, f32[32,1920]{1,0:T(8,128)S(1)}, u32[]{:S(2)}, u32[]{:S(2)}) collective-permute-start(f32[32,1920]{1,0:T(8,128)S(1)} %get-tuple-element.36), channel_id=1, source_target_pairs={{0,32},{32,64},{64,96},{96,0},{128,160},{160,192},{192,224},{224,1... | collective-permute-start | bytes 737288 | tf_op jit(solution)/shard_map/ppermute | solution.py:204
  25.8 7.8 %collective-permute-start.5 = (f32[32,1920]{1,0:T(8,128)S(1)}, f32[32,1920]{1,0:T(8,128)S(1)}, u32[]{:S(2)}, u32[]{:S(2)}) collective-permute-start(f32[32,1920]{1,0:T(8,128)S(1)} %get-tuple-element.37), channel_id=1, source_target_pairs={{32,0},{64,32},{96,64},{0,96},{160,128},{192,160},{224,192},{128,2... | collective-permute-start | bytes 737288 | tf_op jit(solution)/shard_map/ppermute | solution.py:205
  34.5 10.9 %collective-permute-start.6 = (f32[64,1920]{1,0:T(8,128)S(1)}, f32[64,1920]{1,0:T(8,128)S(1)}, u32[]{:S(2)}, u32[]{:S(2)}) collective-permute-start(f32[64,1920]{1,0:T(8,128)S(1)} %get-tuple-element.39), channel_id=1, source_target_pairs={{0,32},{32,64},{64,96},{96,0},{128,160},{160,192},{192,224},{224,1... | collective-permute-start | bytes 1474568 | tf_op jit(solution)/shard_map/ppermute | solution.py:204
  34.8 12.2 %collective-permute-start.7 = (f32[64,1920]{1,0:T(8,128)S(1)}, f32[64,1920]{1,0:T(8,128)S(1)}, u32[]{:S(2)}, u32[]{:S(2)}) collective-permute-start(f32[64,1920]{1,0:T(8,128)S(1)} %get-tuple-element.40), channel_id=1, source_target_pairs={{32,0},{64,32},{96,64},{0,96},{160,128},{192,160},{224,192},{128,2... | collective-permute-start | bytes 1474568 | tf_op jit(solution)/shard_map/ppermute | solution.py:205
  36.5 22.9 %collective-permute-start.10 = (f32[64,1920]{1,0:T(8,128)}, f32[64,1920]{1,0:T(8,128)S(1)}, u32[]{:S(2)}, u32[]{:S(2)}) collective-permute-start(f32[64,1920]{1,0:T(8,128)} %get-tuple-element.45), channel_id=1, source_target_pairs={{0,128},{32,160},{64,192},{96,224},{128,0},{160,32},{192,64},{224,... | collective-permute-start | bytes 1474568 | tf_op jit(solution)/shard_map/ppermute | solution.py:206
  47.8 6.4 %collective-permute-start.8 = (f32[32,1920]{1,0:T(8,128)}, f32[32,1920]{1,0:T(8,128)S(1)}, u32[]{:S(2)}, u32[]{:S(2)}) collective-permute-start(f32[32,1920]{1,0:T(8,128)} %get-tuple-element.43), channel_id=1, source_target_pairs={{0,32},{32,64},{64,96},{96,0},{128,160},{160,192},{192,224},{224,1... | collective-permute-start | bytes 737288 | tf_op jit(solution)/shard_map/ppermute | solution.py:204
  48.1 7.6 %collective-permute-start.9 = (f32[32,1920]{1,0:T(8,128)}, f32[32,1920]{1,0:T(8,128)S(1)}, u32[]{:S(2)}, u32[]{:S(2)}) collective-permute-start(f32[32,1920]{1,0:T(8,128)} %get-tuple-element.44), channel_id=1, source_target_pairs={{32,0},{64,32},{96,64},{0,96},{160,128},{192,160},{224,192},{128,2... | collective-permute-start | bytes 737288 | tf_op jit(solution)/shard_map/ppermute | solution.py:205
  49.8 21.9 %collective-permute-start.15 = (bf16[64,1848]{1,0:T(8,128)(2,1)}, bf16[64,1848]{1,0:T(8,128)(2,1)S(1)}, u32[]{:S(2)}, u32[]{:S(2)}) collective-permute-start(bf16[64,1848]{1,0:T(8,128)(2,1)} %refs_18_.1), channel_id=1, source_target_pairs={{0,1},{1,0},{2,3},{3,2},{4,5},{5,4},{6,7},{7,6},{8,9},{9,8},{10,11... | collective-permute-start | bytes 709640 | tf_op jit(solution)/shard_map/ppermute | solution.py:208
  60.0 13.8 %collective-permute-start.13 = (bf16[64,1920]{1,0:T(8,128)(2,1)S(1)}, bf16[64,1920]{1,0:T(8,128)(2,1)S(1)}, u32[]{:S(2)}, u32[]{:S(2)}) collective-permute-start(bf16[64,1920]{1,0:T(8,128)(2,1)S(1)} %shard_map.109.refs_5_.refs_0_), channel_id=1, source_target_pairs={{0,64},{32,96},{64,0},{96,32},{128,192},{160,224},{192,128},{224,1... | collective-permute-start | bytes 737288 | tf_op jit(solution)/shard_map/ppermute | solution.py:207
  60.9 13.5 %collective-permute-start.12 = (bf16[64,1920]{1,0:T(8,128)(2,1)S(1)}, bf16[64,1920]{1,0:T(8,128)(2,1)S(1)}, u32[]{:S(2)}, u32[]{:S(2)}) collective-permute-start(bf16[64,1920]{1,0:T(8,128)(2,1)S(1)} %shard_map.109.refs_5_.refs_0_), channel_id=1, source_target_pairs={{0,32},{32,64},{64,96},{96,0},{128,160},{160,192},{192,224},{224,1... | collective-permute-start | bytes 737288 | tf_op jit(solution)/shard_map/ppermute | solution.py:204
  63.2 15.9 %collective-permute-start.14 = (bf16[64,1920]{1,0:T(8,128)(2,1)S(1)}, bf16[64,1920]{1,0:T(8,128)(2,1)S(1)}, u32[]{:S(2)}, u32[]{:S(2)}) collective-permute-start(bf16[64,1920]{1,0:T(8,128)(2,1)S(1)} %shard_map.109.refs_5_.refs_0_), channel_id=1, source_target_pairs={{0,128},{32,160},{64,192},{96,224},{128,0},{160,32},{192,64},{224,... | collective-permute-start | bytes 737288 | tf_op jit(solution)/shard_map/ppermute | solution.py:206
  71.7 7.4 %collective-permute-start.11 = (bf16[64,1920]{1,0:T(8,128)(2,1)S(1)}, bf16[64,1920]{1,0:T(8,128)(2,1)S(1)}, u32[]{:S(2)}, u32[]{:S(2)}) collective-permute-start(bf16[64,1920]{1,0:T(8,128)(2,1)S(1)} %shard_map.109.refs_5_.refs_0_), channel_id=1, source_target_pairs={{32,0},{64,32},{96,64},{0,96},{160,128},{192,160},{224,192},{128,2... | collective-permute-start | bytes 737288 | tf_op jit(solution)/shard_map/ppermute | solution.py:205
  72.4 8.8 %collective-permute-start.19 = (bf16[64,1920]{1,0:T(8,128)(2,1)S(1)}, bf16[64,1920]{1,0:T(8,128)(2,1)S(1)}, u32[]{:S(2)}, u32[]{:S(2)}) collective-permute-start(bf16[64,1920]{1,0:T(8,128)(2,1)S(1)} %shard_map.109.refs_5_.refs_0_), channel_id=1, source_target_pairs={{0,1},{1,0},{2,3},{3,2},{4,5},{5,4},{6,7},{7,6},{8,9},{9,8},{10,11... | collective-permute-start | bytes 737288 | tf_op jit(solution)/shard_map/ppermute | solution.py:208
  73.8 9.1 %collective-permute-start.22 = (bf16[64,1920]{1,0:T(8,128)(2,1)S(1)}, bf16[64,1920]{1,0:T(8,128)(2,1)S(1)}, u32[]{:S(2)}, u32[]{:S(2)}) collective-permute-start(bf16[64,1920]{1,0:T(8,128)(2,1)S(1)} %collective-permute-done.13.refs_3_), channel_id=1, source_target_pairs={{0,1},{1,0},{2,3},{3,2},{4,5},{5,4},{6,7},{7,6},{8,9},{9,8},{10,11... | collective-permute-start | bytes 737288 | tf_op jit(solution)/shard_map/ppermute | solution.py:208
  74.4 8.5 %collective-permute-start.21 = (bf16[64,1920]{1,0:T(8,128)(2,1)S(1)}, bf16[64,1920]{1,0:T(8,128)(2,1)S(1)}, u32[]{:S(2)}, u32[]{:S(2)}) collective-permute-start(bf16[64,1920]{1,0:T(8,128)(2,1)S(1)} %collective-permute-done.12.refs_1_.refs_2_), channel_id=1, source_target_pairs={{0,1},{1,0},{2,3},{3,2},{4,5},{5,4},{6,7},{7,6},{8,9},{9,8},{10,11... | collective-permute-start | bytes 737288 | tf_op jit(solution)/shard_map/ppermute | solution.py:208
  79.2 8.0 %collective-permute-start.18 = (bf16[64,1920]{1,0:T(8,128)(2,1)S(1)}, bf16[64,1920]{1,0:T(8,128)(2,1)S(1)}, u32[]{:S(2)}, u32[]{:S(2)}) collective-permute-start(bf16[64,1920]{1,0:T(8,128)(2,1)S(1)} %shard_map.111.refs_4_), channel_id=1, source_target_pairs={{0,64},{32,96},{64,0},{96,32},{128,192},{160,224},{192,128},{224,1... | collective-permute-start | bytes 737288 | tf_op jit(solution)/shard_map/ppermute | solution.py:207
  80.9 9.4 %collective-permute-start.17 = (bf16[64,1920]{1,0:T(8,128)(2,1)S(1)}, bf16[64,1920]{1,0:T(8,128)(2,1)S(1)}, u32[]{:S(2)}, u32[]{:S(2)}) collective-permute-start(bf16[64,1920]{1,0:T(8,128)(2,1)S(1)} %shard_map.111.refs_4_), channel_id=1, source_target_pairs={{0,32},{32,64},{64,96},{96,0},{128,160},{160,192},{192,224},{224,1... | collective-permute-start | bytes 737288 | tf_op jit(solution)/shard_map/ppermute | solution.py:204
  81.3 9.2 %collective-permute-start.16 = (bf16[64,1920]{1,0:T(8,128)(2,1)S(1)}, bf16[64,1920]{1,0:T(8,128)(2,1)S(1)}, u32[]{:S(2)}, u32[]{:S(2)}) collective-permute-start(bf16[64,1920]{1,0:T(8,128)(2,1)S(1)} %shard_map.111.refs_4_), channel_id=1, source_target_pairs={{32,0},{64,32},{96,64},{0,96},{160,128},{192,160},{224,192},{128,2... | collective-permute-start | bytes 737288 | tf_op jit(solution)/shard_map/ppermute | solution.py:205
  82.9 7.9 %collective-permute-start.23 = (bf16[64,1920]{1,0:T(8,128)(2,1)S(1)}, bf16[64,1920]{1,0:T(8,128)(2,1)S(1)}, u32[]{:S(2)}, u32[]{:S(2)}) collective-permute-start(bf16[64,1920]{1,0:T(8,128)(2,1)S(1)} %shard_map.111.refs_4_), channel_id=1, source_target_pairs={{0,1},{1,0},{2,3},{3,2},{4,5},{5,4},{6,7},{7,6},{8,9},{9,8},{10,11... | collective-permute-start | bytes 737288 | tf_op jit(solution)/shard_map/ppermute | solution.py:208
  82.9 7.9 %collective-permute-start.20 = (bf16[64,1920]{1,0:T(8,128)(2,1)S(1)}, bf16[64,1920]{1,0:T(8,128)(2,1)S(1)}, u32[]{:S(2)}, u32[]{:S(2)}) collective-permute-start(bf16[64,1920]{1,0:T(8,128)(2,1)S(1)} %collective-permute-done.11.refs_2_.refs_1_), channel_id=1, source_target_pairs={{0,1},{1,0},{2,3},{3,2},{4,5},{5,4},{6,7},{7,6},{8,9},{9,8},{10,11... | collective-permute-start | bytes 737288 | tf_op jit(solution)/shard_map/ppermute | solution.py:208
  98.2 16.1 %all-to-all-start = ((bf16[16,32,128]{2,1,0:T(8,128)(2,1)}), bf16[16,32,128]{2,1,0:T(8,128)(2,1)S(1)}, u32[]{:S(2)}, u32[]{:S(2)}) async-start(bf16[16,32,128]{2,1,0:T(8,128)(2,1)} %convert_element_type.16), calls=%async_computation | async-start | bytes 262144 | tf_op jit(solution)/shard_map/all_to_all | solution.py:248
  (23 other events, 173.4 us)
